TPU v7x, 32 devices: a whole 2x2x4 slice. The times are simulated.
32 devices in a mesh: seq: 8 (over y, x, core), head: 4 (over z).
Axes of the slice: x: 2, y: 2, z: 4, core: 2. Of those that a mesh axis runs over, the one named last changes fastest.
Arguments:
- queries: bfloat16 [4096, 8192], P('seq', 'head'), may hold values from -0.9 to 0.9
- keys: bfloat16 [4096, 8192], P('seq', 'head'), may hold values from -0.9 to 0.9
- values: bfloat16 [4096, 8192], P('seq', 'head'), may hold values from -0.9 to 0.9
- grad_out: bfloat16 [4096, 8192], P('seq', 'head'), may hold values from -0.9 to 0.9
- rates: float32 [64], P('head'), may hold values from 0.00012207031 to 0.04
- doc_lengths: int32 [8], replicated, may hold values from 1 to 3072, 4096 in all
Outputs:
- grad_queries: bfloat16 [4096, 8192], P(('seq', 'head'))
- grad_keys: bfloat16 [4096, 8192], P(('seq', 'head'))
- grad_values: bfloat16 [4096, 8192], P(('seq', 'head'))
Inputs may be any that keep to these rules, and one draw needn't show every extreme that they name: `doc_lengths`: lengths of the completions in order, summing to 4096; the longest has exactly 3072 tokens.
All inputs are finite; a program needn't handle non-finite values.
Results may differ from a plain program's by a relative error of at most 0.001.
The roundings to bfloat16 on the way count: a program that leaves them out, or rounds other values in their place, can miss the bound.
Values may be sent and summed in bfloat16 or wider, within the bound.
A program may use at most 128 MiB of HBM per device.

v0:
```python
import jax
import jax.numpy as jnp
from jax import lax
from jax.sharding import PartitionSpec as P


def seg_ids(doc_lengths, positions):
    starts = jnp.cumsum(doc_lengths, dtype=jnp.int32) - doc_lengths
    inside = (starts[None, :] <= positions[:, None]).astype(jnp.int32)
    return jnp.sum(inside, axis=1, dtype=jnp.int32) - 1


def body(queries, keys, values, grad_out, rates, doc_lengths):
    length = queries.shape[0]
    heads_here = rates.shape[0]
    head_dim = queries.shape[1] // heads_here
    query_rows = queries.reshape(length, heads_here, head_dim)
    key_rows = keys.reshape(length, heads_here, head_dim)
    value_rows = values.reshape(length, heads_here, head_dim)
    grad_rows = grad_out.reshape(length, heads_here, head_dim)
    shard = lax.axis_index("seq")
    shards = lax.axis_size("seq")
    first_pos = shard * length
    positions = first_pos + jnp.arange(length, dtype=jnp.int32)
    segment = seg_ids(doc_lengths, positions)
    edges = seg_ids(doc_lengths, jnp.stack([first_pos - 1, first_pos + length]))
    seg_prev = edges[0]
    seg_next = edges[1]
    offsets = jnp.arange(length, dtype=jnp.float32)
    weight_k = jnp.where(
        (segment == segment[-1])[:, None],
        jnp.exp(-rates[None, :] * (length - 1.0 - offsets)[:, None]),
        0.0,
    )
    weighted_k = (key_rows.astype(jnp.float32) * weight_k[:, :, None]).astype(jnp.bfloat16)
    summary_fwd = jnp.einsum(
        "uhd,uhe->hde", weighted_k, value_rows, preferred_element_type=jnp.float32
    )
    weight_q = jnp.where(
        (segment == segment[0])[:, None], jnp.exp(-rates[None, :] * offsets[:, None]), 0.0
    )
    weighted_q = (query_rows.astype(jnp.float32) * weight_q[:, :, None]).astype(jnp.bfloat16)
    summary_bwd = jnp.einsum(
        "thd,the->hde", weighted_q, grad_rows, preferred_element_type=jnp.float32
    )
    gathered_fwd, gathered_bwd = (
        lax.all_gather(summary_fwd[None], "seq", axis=0, tiled=True),
        lax.all_gather(summary_bwd[None], "seq", axis=0, tiled=True),
    )
    blocks_all = jnp.arange(shards, dtype=jnp.int32)
    firsts = blocks_all * length
    breaks_fwd = (
        seg_ids(doc_lengths, firsts + length - 1) != seg_ids(doc_lengths, firsts - 1)
    ).astype(jnp.int32)
    breaks_bwd = (seg_ids(doc_lengths, firsts) != seg_ids(doc_lengths, firsts + length)).astype(
        jnp.int32
    )
    count_fwd = jnp.cumsum(breaks_fwd, dtype=jnp.int32)
    count_bwd = jnp.cumsum(breaks_bwd, dtype=jnp.int32)
    before_here = jnp.sum(jnp.where(blocks_all == shard - 1, count_fwd, 0), dtype=jnp.int32)
    valid_fwd = (blocks_all < shard) & (before_here - count_fwd == 0)
    gap_fwd = jnp.maximum(shard - 1 - blocks_all, 0).astype(jnp.float32)
    mixing_fwd = jnp.where(
        valid_fwd[:, None], jnp.exp(-rates[None, :] * length * gap_fwd[:, None]), 0.0
    )
    state_in = jnp.einsum("ih,ihde->hde", mixing_fwd, gathered_fwd, precision=lax.Precision.HIGHEST)
    here_bwd = jnp.sum(jnp.where(blocks_all == shard, count_bwd, 0), dtype=jnp.int32)
    valid_bwd = (blocks_all > shard) & (count_bwd - breaks_bwd - here_bwd == 0)
    gap_bwd = jnp.maximum(blocks_all - 1 - shard, 0).astype(jnp.float32)
    mixing_bwd = jnp.where(
        valid_bwd[:, None], jnp.exp(-rates[None, :] * length * gap_bwd[:, None]), 0.0
    )
    back_in = jnp.einsum("ih,ihde->hde", mixing_bwd, gathered_bwd, precision=lax.Precision.HIGHEST)
    distance = offsets[:, None] - offsets[None, :]
    allowed = (segment[:, None] == segment[None, :]) & (distance >= 0)
    decayed = jnp.where(
        allowed[None], jnp.exp(-rates[:, None, None] * jnp.maximum(distance, 0.0)[None]), 0.0
    )
    scores_gv = jnp.einsum(
        "the,uhe->htu", grad_rows, value_rows, preferred_element_type=jnp.float32
    )
    scores_qk = jnp.einsum("thd,uhd->htu", query_rows, key_rows, preferred_element_type=jnp.float32)
    weights_p = (decayed * scores_gv).astype(jnp.bfloat16)
    weights_a = (decayed * scores_qk).astype(jnp.bfloat16)
    local_q = jnp.einsum("htu,uhd->thd", weights_p, key_rows, preferred_element_type=jnp.float32)
    local_k = jnp.einsum("htu,thd->uhd", weights_p, query_rows, preferred_element_type=jnp.float32)
    local_v = jnp.einsum("htu,the->uhe", weights_a, grad_rows, preferred_element_type=jnp.float32)
    factor_in = jnp.where(
        (segment == seg_prev)[:, None], jnp.exp(-rates[None, :] * (offsets + 1.0)[:, None]), 0.0
    )
    factor_back = jnp.where(
        (segment == seg_next)[:, None], jnp.exp(-rates[None, :] * (length - offsets)[:, None]), 0.0
    )
    state_b = state_in.astype(jnp.bfloat16)
    back_b = back_in.astype(jnp.bfloat16)
    outer_q = (
        jnp.einsum("the,hde->thd", grad_rows, state_b, preferred_element_type=jnp.float32)
        * factor_in[:, :, None]
    )
    outer_k = (
        jnp.einsum("the,hde->thd", value_rows, back_b, preferred_element_type=jnp.float32)
        * factor_back[:, :, None]
    )
    outer_v = (
        jnp.einsum("thd,hde->the", key_rows, back_b, preferred_element_type=jnp.float32)
        * factor_back[:, :, None]
    )
    grad_q = (local_q + outer_q).astype(jnp.bfloat16).reshape(length, heads_here * head_dim)
    grad_k = (local_k + outer_k).astype(jnp.bfloat16).reshape(length, heads_here * head_dim)
    grad_v = (local_v + outer_v).astype(jnp.bfloat16).reshape(length, heads_here * head_dim)
    grad_queries, grad_keys, grad_values = (
        lax.all_to_all(grad_q, "head", split_axis=0, concat_axis=1, tiled=True),
        lax.all_to_all(grad_k, "head", split_axis=0, concat_axis=1, tiled=True),
        lax.all_to_all(grad_v, "head", split_axis=0, concat_axis=1, tiled=True),
    )
    return (grad_queries, grad_keys, grad_values)


def solution(mesh):
    return jax.shard_map(
        body,
        mesh=mesh,
        in_specs=(
            P("seq", "head"),
            P("seq", "head"),
            P("seq", "head"),
            P("seq", "head"),
            P("head"),
            P(),
        ),
        out_specs=(P(("seq", "head"), None), P(("seq", "head"), None), P(("seq", "head"), None)),
        check_vma=False,
    )
```

profile of v0, /device:TPU:0, one launch (start us, length us, event | category | flops | bytes accessed | tf_op | source)
XLA Modules:
  0.0 279.2 jit_solution(4618540090170749993)
XLA Ops:
  21.2 3.9 %copy.152 = bf16[512,2048]{0,1:T(8,128)(2,1)} copy(bf16[512,2048]{1,0:T(8,128)(2,1)} %param.7) | data formatting | bytes 4194304 | tf_op jit(solution)/shard_map/reshape | solution.py:18
  25.1 4.1 %fusion.8 = f32[16,128,128]{2,1,0:T(8,128)} fusion(bf16[512,16,128]{0,2,1:T(8,128)(2,1)} %bitcast.116, f32[512,16]{0,1:T(8,128)S(1)} %get-tuple-element.26, bf16[512,2048]{1,0:T(8,128)(2,1)} %param.8), kind=kOutput, calls=%fused_computation.17 | convolution fusion | flops 271581184 | bytes 5275648 | tf_op jit(solution)/shard_map/uhd,uhe->hde/dot_general | solution.py:36
  32.9 10.3 %fusion.13 = f32[16,512,128]{2,1,0:T(8,128)} fusion(bf16[512,16,128]{0,2,1:T(8,128)(2,1)} %bitcast.121, bf16[512,16,128]{0,2,1:T(8,128)(2,1)} %bitcast.117, f32[512,512]{1,0:T(8,128)S(1)} %fusion.27, f32[16]{0:T(128)S(1)} %get-tuple-element.31, pred[512,512]{1,0:T(8,128)(4,1)S(1)} %fusion.29, bf16[512,2048]{1,0:T(8,128)(2,1)S(1)} %copy-done), kind=kOutput, calls=%fused_computation.22 | convolution fusion | flops 2164260864 | bytes 11796544 | tf_op jit(solution)/shard_map/htu,the->uhe/dot_general | solution.py:87
  43.3 35.1 %all-gather.7.cloned.1.call-done = f32[128,128,128]{2,1,0:T(8,128)} async-done(((f32[16,128,128]{2,1,0:T(8,128)}), f32[128,128,128]{2,1,0:T(8,128)}) %all-gather.7.cloned.1.call-update) | async-done | bytes 8388624 | tf_op jit(solution)/shard_map/all_gather | solution.py:48
  78.4 4.1 %multiply_reduce_fusion = bf16[16,128,128]{2,1,0:T(8,128)(2,1)S(1)} fusion(f32[16,8,128,128]{3,2,0,1:T(8,128)} %bitcast.124, f32[16,8]{0,1:T(8,128)S(1)} %get-tuple-element.22), kind=kLoop, calls=%fused_computation.3 | loop fusion | flops 3932160 | bytes 8913408
  89.3 4.3 %all_to_all.50 = bf16[4,128,2048]{2,1,0:T(8,128)(2,1)} reshape(bf16[512,16,128]{2,1,0:T(8,128)(2,1)} %copy.130) | data formatting | bytes 4194304 | tf_op jit(solution)/shard_map/all_to_all | solution.py:114
  93.6 4.6 %all-to-all-start.2 = ((bf16[4,128,2048]{2,1,0:T(8,128)(2,1)}), bf16[4,128,2048]{2,1,0:T(8,128)(2,1)}, u32[]{:S(2)}, u32[]{:S(2)}) async-start(bf16[4,128,2048]{2,1,0:T(8,128)(2,1)} %all_to_all.50), calls=%async_computation.2 | async-start | bytes 4194304 | tf_op jit(solution)/shard_map/all_to_all | solution.py:114
  98.3 6.2 %multiply_convert_fusion.1 = bf16[16,512,512]{2,1,0:T(8,128)(2,1)S(1)} fusion(f32[512,512]{1,0:T(8,128)} %copy-done.5, f32[16]{0:T(128)S(1)} %get-tuple-element.31, pred[512,512]{1,0:T(8,128)(4,1)S(1)} %fusion.29, bf16[512,2048]{1,0:T(8,128)(2,1)} %param.8, bf16[512,2048]{1,0:T(8,128)(2,1)S(1)} %copy-done), kind=kOutput, calls=%fused_computation.1 | convolution fusion | flops 1090519040 | bytes 13893696 | tf_op jit(solution)/shard_map/the,uhe->htu/dot_general | solution.py:79
  107.7 4.4 %fusion.42 = f32[16,512,128]{2,1,0:T(8,128)} fusion(bf16[16,512,512]{2,1,0:T(8,128)(2,1)S(1)} %multiply_convert_fusion.1, bf16[512,16,128]{0,2,1:T(8,128)(2,1)S(1)} %bitcast.119), kind=kOutput, calls=%fused_computation.91 | convolution fusion | flops 1073741824 | bytes 14680064 | tf_op jit(solution)/shard_map/htu,uhd->thd/dot_general | solution.py:85
  112.1 22.7 %all-gather.5.cloned.1.call-done = f32[128,128,128]{2,1,0:T(8,128)} async-done(((f32[16,128,128]{2,1,0:T(8,128)}), f32[128,128,128]{2,1,0:T(8,128)}) %all-gather.5.cloned.1.call-update) | async-done | bytes 8388624 | tf_op jit(solution)/shard_map/all_gather | solution.py:47
  134.7 15.5 %fusion = f32[16,1,128,128]{3,1,2,0:T(1,128)S(1)} fusion(f32[8,16,1,1]{0,2,3,1:T(1,128)S(1)} %copy.135, f32[8,16,128,128]{3,2,1,0:T(8,128)} %bitcast.123), kind=kOutput, calls=%fused_computation.4 | convolution fusion | flops 25165824 | bytes 9437696 | tf_op jit(solution)/shard_map/ih,ihde->hde/dot_general | solution.py:66
  154.5 4.2 %all_to_all.42 = bf16[4,128,2048]{2,1,0:T(8,128)(2,1)} reshape(bf16[512,16,128]{2,1,0:T(8,128)(2,1)} %copy.113) | data formatting | bytes 4194304 | tf_op jit(solution)/shard_map/all_to_all | solution.py:112
  158.6 4.6 %all-to-all-start = ((bf16[4,128,2048]{2,1,0:T(8,128)(2,1)}), bf16[4,128,2048]{2,1,0:T(8,128)(2,1)}, u32[]{:S(2)}, u32[]{:S(2)}) async-start(bf16[4,128,2048]{2,1,0:T(8,128)(2,1)} %all_to_all.42), calls=%async_computation | async-start | bytes 4194304 | tf_op jit(solution)/shard_map/all_to_all | solution.py:112
  163.2 6.6 %fusion.43 = f32[16,512,128]{2,1,0:T(8,128)S(1)} fusion(bf16[16,512,512]{2,1,0:T(8,128)(2,1)} %copy-done.1, bf16[512,16,128]{0,2,1:T(8,128)(2,1)} %bitcast.122), kind=kOutput, calls=%fused_computation.92 | convolution fusion | flops 1073741824 | bytes 14680064 | tf_op jit(solution)/shard_map/htu,thd->uhd/dot_general | solution.py:86
  174.4 4.2 %all_to_all.46 = bf16[4,128,2048]{2,1,0:T(8,128)(2,1)} reshape(bf16[512,16,128]{2,1,0:T(8,128)(2,1)} %copy.122) | data formatting | bytes 4194304 | tf_op jit(solution)/shard_map/all_to_all | solution.py:113
  178.5 33.5 %all-to-all-done = bf16[4,128,2048]{2,1,0:T(8,128)(2,1)} async-done(((bf16[4,128,2048]{2,1,0:T(8,128)(2,1)}), bf16[4,128,2048]{2,1,0:T(8,128)(2,1)}, u32[]{:S(2)}, u32[]{:S(2)}) %all-to-all-start) | async-done | bytes 2097184 | tf_op jit(solution)/shard_map/all_to_all | solution.py:112
  212.0 4.4 %all-to-all-start.1 = ((bf16[4,128,2048]{2,1,0:T(8,128)(2,1)}), bf16[4,128,2048]{2,1,0:T(8,128)(2,1)}, u32[]{:S(2)}, u32[]{:S(2)}) async-start(bf16[4,128,2048]{2,1,0:T(8,128)(2,1)} %all_to_all.46), calls=%async_computation.1 | async-start | bytes 4194304 | tf_op jit(solution)/shard_map/all_to_all | solution.py:113
  216.5 3.9 %copy.131 = bf16[128,4,2048]{0,2,1:T(8,128)(2,1)} copy(bf16[128,4,2048]{2,0,1:T(8,128)(2,1)} %bitcast.30) | data formatting | bytes 4194304 | tf_op jit(solution)/shard_map/all_to_all | solution.py:114
  220.4 4.1 %copy.134 = bf16[128,8192]{1,0:T(8,128)(2,1)} copy(bf16[128,8192]{0,1:T(8,128)(2,1)} %bitcast.125) | data formatting | bytes 4194304
  224.5 3.9 %copy.114 = bf16[128,4,2048]{0,2,1:T(8,128)(2,1)} copy(bf16[128,4,2048]{2,0,1:T(8,128)(2,1)} %bitcast.16) | data formatting | bytes 4194304 | tf_op jit(solution)/shard_map/all_to_all | solution.py:112
  228.4 4.1 %copy.132 = bf16[128,8192]{1,0:T(8,128)(2,1)} copy(bf16[128,8192]{0,1:T(8,128)(2,1)} %bitcast.126) | data formatting | bytes 4194304
  232.5 31.9 %all-to-all-done.1 = bf16[4,128,2048]{2,1,0:T(8,128)(2,1)} async-done(((bf16[4,128,2048]{2,1,0:T(8,128)(2,1)}), bf16[4,128,2048]{2,1,0:T(8,128)(2,1)}, u32[]{:S(2)}, u32[]{:S(2)}) %all-to-all-start.1) | async-done | bytes 2097184 | tf_op jit(solution)/shard_map/all_to_all | solution.py:113
  264.4 3.9 %copy.123 = bf16[128,4,2048]{0,2,1:T(8,128)(2,1)} copy(bf16[128,4,2048]{2,0,1:T(8,128)(2,1)} %bitcast.26) | data formatting | bytes 4194304 | tf_op jit(solution)/shard_map/all_to_all | solution.py:113
  268.3 4.1 %copy.133 = bf16[128,8192]{1,0:T(8,128)(2,1)} copy(bf16[128,8192]{0,1:T(8,128)(2,1)} %bitcast.127) | data formatting | bytes 4194304
  (58 shorter events, 36.5 us)
Async XLA Ops:
  7.2 10.6 %copy-start = (bf16[512,2048]{1,0:T(8,128)(2,1)S(1)}, bf16[512,2048]{1,0:T(8,128)(2,1)}, u32[]{:S(2)}) copy-start(bf16[512,2048]{1,0:T(8,128)(2,1)} %param.9) | copy-start | bytes 6291460
  7.2 71.2 %all-gather.7.cloned.1.call-start = ((), (), s32[]{:S(2)}) async-start(), calls=%async_computation.4 | async-start | bytes 9437184 | tf_op jit(solution)/shard_map/all_gather | solution.py:48
  21.1 113.6 %all-gather.5.cloned.1.call-start = ((), (), s32[]{:S(2)}) async-start(), calls=%async_computation.3 | async-start | bytes 9437184 | tf_op jit(solution)/shard_map/all_gather | solution.py:47
  31.3 12.0 %copy-start.5 = (f32[512,512]{1,0:T(8,128)}, f32[512,512]{1,0:T(8,128)S(1)}, u32[]{:S(2)}) copy-start(f32[512,512]{1,0:T(8,128)S(1)} %fusion.27) | copy-start | bytes 3145732
  93.6 65.0 %all-to-all-start.2 = ((bf16[4,128,2048]{2,1,0:T(8,128)(2,1)}), bf16[4,128,2048]{2,1,0:T(8,128)(2,1)}, u32[]{:S(2)}, u32[]{:S(2)}) async-start(bf16[4,128,2048]{2,1,0:T(8,128)(2,1)} %all_to_all.50), calls=%async_computation.2 | async-start | bytes 4194304 | tf_op jit(solution)/shard_map/all_to_all | solution.py:114
  98.3 9.4 %copy-start.2 = (bf16[512,2048]{0,1:T(8,128)(2,1)S(1)}, bf16[512,2048]{0,1:T(8,128)(2,1)}, u32[]{:S(2)}) copy-start(bf16[512,2048]{0,1:T(8,128)(2,1)} %copy.152) | copy-start | bytes 6291460
  104.5 3.3 %copy-start.1 = (bf16[16,512,512]{2,1,0:T(8,128)(2,1)}, bf16[16,512,512]{2,1,0:T(8,128)(2,1)S(1)}, u32[]{:S(2)}) copy-start(bf16[16,512,512]{2,1,0:T(8,128)(2,1)S(1)} %multiply_convert_fusion.1) | copy-start | bytes 25165828
  134.7 15.5 %copy-start.3 = (f32[16,512,128]{2,1,0:T(8,128)S(1)}, f32[16,512,128]{2,1,0:T(8,128)}, u32[]{:S(2)}) copy-start(f32[16,512,128]{2,1,0:T(8,128)} %fusion.42) | copy-start | bytes 12582916
  158.6 53.4 %all-to-all-start = ((bf16[4,128,2048]{2,1,0:T(8,128)(2,1)}), bf16[4,128,2048]{2,1,0:T(8,128)(2,1)}, u32[]{:S(2)}, u32[]{:S(2)}) async-start(bf16[4,128,2048]{2,1,0:T(8,128)(2,1)} %all_to_all.42), calls=%async_computation | async-start | bytes 4194304 | tf_op jit(solution)/shard_map/all_to_all | solution.py:112
  163.2 6.6 %copy-start.4 = (bf16[512,2048]{1,0:T(8,128)(2,1)S(1)}, bf16[512,2048]{1,0:T(8,128)(2,1)}, u32[]{:S(2)}) copy-start(bf16[512,2048]{1,0:T(8,128)(2,1)} %param.8) | copy-start | bytes 6291460
  212.0 52.4 %all-to-all-start.1 = ((bf16[4,128,2048]{2,1,0:T(8,128)(2,1)}), bf16[4,128,2048]{2,1,0:T(8,128)(2,1)}, u32[]{:S(2)}, u32[]{:S(2)}) async-start(bf16[4,128,2048]{2,1,0:T(8,128)(2,1)} %all_to_all.46), calls=%async_computation.1 | async-start | bytes 4194304 | tf_op jit(solution)/shard_map/all_to_all | solution.py:113
Sparse Core Ops, SparseCore 0:
  21.2 57.1 all-gather.6
  80.3 54.3 all-gather.4
where the time goes:
time: 280 us; the launch traced here: 279 us
  waiting for transfers between devices  123 us (44%)
  matrix products  57.5 us (21%)
  local copies, waits for them, and re-layouts  57.4 us (20%)
  between operations  14.3 us (5%)
  starting transfers between devices  13.7 us (5%)
  other arithmetic  13.1 us (5%)
    all_gather x1, waiting for transfers between devices, body(): lax.all_gather(summary_bwd[None], 'seq', axis=0, tiled=True)  35.1 us
    all_to_all x1, waiting for transfers between devices, body(): lax.all_to_all(grad_q, 'head', split_axis=0, concat_axis=1, tiled=True)  33.5 us
    all_to_all x1, waiting for transfers between devices, body(): lax.all_to_all(grad_k, 'head', split_axis=0, concat_axis=1, tiled=True)  31.9 us
    all_gather x1, waiting for transfers between devices, body(): lax.all_gather(summary_fwd[None], 'seq', axis=0, tiled=True)  22.7 us
    unnamed x15, local copies, waits for them, and re-layouts  15.5 us
    dot_general x1, matrix products, body(): jnp.einsum('ih,ihde->hde', mixing_fwd, gathered_fwd, precision=lax.Precis...  15.5 us
    dot_general x1, matrix products, body(): jnp.einsum('htu,the->uhe', weights_a, grad_rows, preferred_element_type=j...  10.3 us
    all_to_all x2, local copies, waits for them, and re-layouts, body(): lax.all_to_all(grad_v, 'head', split_axis=0, concat_axis=1, tiled=True)  8.25 us
  transfers between devices with their start and end apart: 5, of which 4 were waited for; matrix products, arithmetic and copies ran while one was open for 32% of the time, Pallas kernels for 0%

commit v1 on v0

v1 whole, which is shorter than its diff:
```python
import functools

import jax
import jax.numpy as jnp
from jax import lax
from jax.experimental import pallas as pl
from jax.experimental.pallas import tpu as pltpu
from jax.sharding import PartitionSpec as P

MESH = pl.DeviceIdType.MESH
NEVER = 1e30
LEAD = 3


def dot(a, b, dims):
    return lax.dot_general(a, b, (dims, ((), ())), preferred_element_type=jnp.float32)


NN = ((1,), (0,))
NT = ((1,), (1,))
TN = ((0,), (0,))


def kernel(
    shards,
    groups,
    docs,
    lengths,
    rates,
    q_hbm,
    k_hbm,
    v_hbm,
    g_hbm,
    dq_hbm,
    dk_hbm,
    dv_hbm,
    rows_in,
    dist,
    row_dist,
    sums,
    gathered,
    acc,
    stage,
    land,
    gaps,
    load_sem,
    sum_send,
    sum_recv,
    out_send,
    out_recv,
    write_sem,
):
    heads, _, length, head_dim = rows_in.shape
    part = length // groups
    shard = lax.axis_index("seq")
    group = lax.axis_index("head")
    inputs = (q_hbm, k_hbm, v_hbm, g_hbm)
    outputs = (dq_hbm, dk_hbm, dv_hbm)

    def load(h):
        columns = pl.ds(pl.multiple_of(h * head_dim, head_dim), head_dim)
        return [
            pltpu.make_async_copy(ref.at[:, columns], rows_in.at[h, i], load_sem.at[h])
            for i, ref in enumerate(inputs)
        ]

    @pl.loop(0, heads)
    def _(h):
        for copy in load(h):
            copy.start()

    barrier = pltpu.get_barrier_semaphore()
    for d in range(1, shards):
        peer = lax.rem(shard + d, shards)
        pl.semaphore_signal(barrier, inc=1, device_id=(peer, group), device_id_type=MESH)
    for d in range(1, groups):
        peer = lax.rem(group + d, groups)
        pl.semaphore_signal(barrier, inc=1, device_id=(shard, peer), device_id_type=MESH)

    first = shard * length

    def starts():
        total = jnp.int32(0)
        for i in range(docs):
            yield total
            total = total + lengths[i]

    def seg(positions):
        count = -1
        for start in starts():
            count = count + jnp.where(start <= positions, 1, 0)
        return count

    seg_first = seg(first)
    seg_last = seg(first + length - 1)
    seg_prev = seg(first - 1)
    seg_next = seg(first + length)
    wide = (length, head_dim)
    offset = lax.broadcasted_iota(jnp.int32, wide, 0)
    segment = seg(first + offset)
    where = offset.astype(jnp.float32)
    row_dist[0] = jnp.where(segment == seg_last, length - 1.0 - where, NEVER)
    row_dist[1] = jnp.where(segment == seg_first, where, NEVER)
    row_dist[2] = jnp.where(segment == seg_prev, where + 1.0, NEVER)
    row_dist[3] = jnp.where(segment == seg_next, length - where, NEVER)

    def summarise(h):
        pltpu.make_async_copy(rows_in.at[h], rows_in.at[h], load_sem.at[h]).wait()
        rate = rates[h]
        weighted_k = (
            rows_in[h, 1].astype(jnp.float32) * jnp.exp(-rate * row_dist[0])
        ).astype(jnp.bfloat16)
        sums[0, h] = dot(weighted_k, rows_in[h, 2], TN)
        weighted_q = (
            rows_in[h, 0].astype(jnp.float32) * jnp.exp(-rate * row_dist[1])
        ).astype(jnp.bfloat16)
        sums[1, h] = dot(weighted_q, rows_in[h, 3], TN)

    def send_sums(h):
        for d in range(1, shards):
            peer = lax.rem(shard + d, shards)
            back = (shard + d) // shards
            pltpu.make_async_remote_copy(
                src_ref=sums.at[back, h],
                dst_ref=gathered.at[h, d - 1],
                send_sem=sum_send.at[h],
                recv_sem=sum_recv.at[h],
                device_id=(peer, group),
                device_id_type=MESH,
            ).start()

    summarise(0)
    pl.semaphore_wait(barrier, shards + groups - 2)
    send_sums(0)

    for d in range(1, shards):
        source = lax.rem(shard - d + shards, shards)
        ahead = (shard + shards - d) // shards
        same_fwd = seg((source + 1) * length - 1) == seg_prev
        same_bwd = seg(source * length) == seg_next
        gaps[0, d - 1] = jnp.where(
            jnp.logical_and(ahead == 1, same_fwd), float(length * (d - 1)), NEVER
        )
        gaps[1, d - 1] = jnp.where(
            jnp.logical_and(ahead == 0, same_bwd), float(length * (shards - d - 1)), NEVER
        )

    lead = min(LEAD, heads)
    for h in range(1, lead):
        summarise(h)
        send_sums(h)

    tile = min(256, length)
    tiles = length // tile
    across = lax.broadcasted_iota(jnp.int32, (1, length), 1)
    seg_across = seg(first + across)
    for i in range(tiles):
        down = i * tile + lax.broadcasted_iota(jnp.int32, (tile, 1), 0)
        seg_down = seg(first + down)
        gap = down - across
        dist[pl.ds(i * tile, tile), :] = jnp.where(
            jnp.logical_and(seg_down == seg_across, gap >= 0), gap.astype(jnp.float32), NEVER
        )

    order = sorted(range(1, groups), key=lambda d: abs(2 * d - groups))

    def own(h):
        columns = pl.ds(pl.multiple_of((group * heads + h) * head_dim, head_dim), head_dim)
        return [
            pltpu.make_async_copy(stage.at[h, group, c], ref.at[:, columns], write_sem)
            for c, ref in enumerate(outputs)
        ]

    def push(h, d):
        peer = lax.rem(group + d, groups)
        return pltpu.make_async_remote_copy(
            src_ref=stage.at[h, peer],
            dst_ref=land.at[d - 1, h],
            send_sem=out_send,
            recv_sem=out_recv.at[d - 1, h],
            device_id=(shard, peer),
            device_id_type=MESH,
        )

    @pl.loop(0, heads)
    def _(h):
        @pl.when(h + lead < heads)
        def _():
            summarise(h + lead)
            send_sums(h + lead)

        rate = rates[h]
        for i in range(tiles):
            rows, seen = pl.ds(i * tile, tile), (i + 1) * tile
            q, g = rows_in[h, 0, rows], rows_in[h, 3, rows]
            k, v = rows_in[h, 1, pl.ds(0, seen)], rows_in[h, 2, pl.ds(0, seen)]
            decay = jnp.exp(-rate * dist[rows, pl.ds(0, seen)])
            p = (decay * dot(g, v, NT)).astype(jnp.bfloat16)
            a = (decay * dot(q, k, NT)).astype(jnp.bfloat16)
            acc[0, rows] = dot(p, k, NN)
            dk, dv = dot(p, q, TN), dot(a, g, TN)
            if i:
                acc[1, pl.ds(0, i * tile)] += dk[: i * tile]
                acc[2, pl.ds(0, i * tile)] += dv[: i * tile]
            acc[1, rows] = dk[i * tile :]
            acc[2, rows] = dv[i * tile :]

        pltpu.make_async_copy(gathered.at[h], gathered.at[h], sum_recv.at[h]).wait()
        state = jnp.zeros((head_dim, head_dim), jnp.float32)
        back = jnp.zeros((head_dim, head_dim), jnp.float32)
        for d in range(shards - 1):
            summary = gathered[h, d]
            state += jnp.exp(jnp.full((1, head_dim), -rate * gaps[0, d])) * summary
            back += jnp.exp(jnp.full((1, head_dim), -rate * gaps[1, d])) * summary
        state = state.astype(jnp.bfloat16)
        back = back.astype(jnp.bfloat16)
        factor_in = jnp.exp(-rate * row_dist[2])
        factor_back = jnp.exp(-rate * row_dist[3])
        dq = acc[0] + dot(rows_in[h, 3], state, NT) * factor_in
        dk = acc[1] + dot(rows_in[h, 2], back, NT) * factor_back
        dv = acc[2] + dot(rows_in[h, 1], back, NN) * factor_back
        for c, total in enumerate((dq, dk, dv)):
            stage[h, :, c] = total.astype(jnp.bfloat16).reshape(groups, part, head_dim)
        for d in order:
            push(h, d).start()
        for copy in own(h):
            copy.start()

    def landed(h, d):
        source = lax.rem(group - d + groups, groups)
        columns = pl.ds(pl.multiple_of((source * heads + h) * head_dim, head_dim), head_dim)
        return [
            pltpu.make_async_copy(land.at[d - 1, h, c], ref.at[:, columns], write_sem)
            for c, ref in enumerate(outputs)
        ]

    @pl.loop(0, heads)
    def _(h):
        for d in order:
            push(h, d).wait_recv()
            for copy in landed(h, d):
                copy.start()

    @pl.loop(0, heads)
    def _(h):
        pltpu.make_async_copy(gathered.at[h], gathered.at[h], sum_send.at[h]).wait()

    pltpu.make_async_copy(land, land, out_send).wait()
    pltpu.make_async_copy(stage, stage, write_sem).wait()


def body(queries, keys, values, grad_out, rates, doc_lengths):
    length, columns = queries.shape
    heads = rates.shape[0]
    head_dim = columns // heads
    shards = lax.axis_size("seq")
    groups = lax.axis_size("head")
    part = length // groups
    docs = doc_lengths.shape[0]
    smem = pl.BlockSpec(memory_space=pltpu.SMEM)
    hbm = pl.BlockSpec(memory_space=pl.ANY)
    bf16, f32 = jnp.bfloat16, jnp.float32
    out = jax.ShapeDtypeStruct((part, groups * columns), bf16)
    return pl.pallas_call(
        functools.partial(kernel, shards, groups, docs),
        out_shape=(out, out, out),
        in_specs=[smem, smem, hbm, hbm, hbm, hbm],
        out_specs=(hbm, hbm, hbm),
        scratch_shapes=[
            pltpu.VMEM((heads, 4, length, head_dim), bf16),
            pltpu.VMEM((length, length), f32),
            pltpu.VMEM((4, length, head_dim), f32),
            pltpu.VMEM((2, heads, head_dim, head_dim), f32),
            pltpu.VMEM((heads, shards - 1, head_dim, head_dim), f32),
            pltpu.VMEM((3, length, head_dim), f32),
            pltpu.VMEM((heads, groups, 3, part, head_dim), bf16),
            pltpu.VMEM((groups - 1, heads, 3, part, head_dim), bf16),
            pltpu.SMEM((2, shards - 1), f32),
            pltpu.SemaphoreType.DMA((heads,)),
            pltpu.SemaphoreType.DMA((heads,)),
            pltpu.SemaphoreType.DMA((heads,)),
            pltpu.SemaphoreType.DMA,
            pltpu.SemaphoreType.DMA((groups - 1, heads)),
            pltpu.SemaphoreType.DMA,
        ],
        compiler_params=pltpu.CompilerParams(
            collective_id=0, has_side_effects=True, vmem_limit_bytes=48 * 1024 * 1024
        ),
        cost_estimate=pl.CostEstimate(
            flops=heads * length * (10 * length + 10 * head_dim) * head_dim,
            bytes_accessed=7 * length * columns * 2,
            transcendentals=heads * length * (length + 4 * head_dim),
        ),
    )(doc_lengths, rates, queries, keys, values, grad_out)


def solution(mesh):
    return jax.shard_map(
        body,
        mesh=mesh,
        in_specs=(
            P("seq", "head"),
            P("seq", "head"),
            P("seq", "head"),
            P("seq", "head"),
            P("head"),
            P(),
        ),
        out_specs=(P(("seq", "head"), None), P(("seq", "head"), None), P(("seq", "head"), None)),
        check_vma=False,
    )
```

time: 280 us -> 157 us (0.56)
  Pallas kernels: 0 us -> 149 us
  waiting for transfers between devices: 123 us -> 0 us
  matrix products: 57.5 us -> 0 us
  local copies, waits for them, and re-layouts: 57.4 us -> 6.29 us
  starting transfers between devices: 13.7 us -> 0 us
  between operations: 14.3 us -> 0.65 us
  other arithmetic: 13.1 us -> 0 us
    pallas_call x0 -> x1, Pallas kernels: none -> 149 us  [body(): pl.pallas_call(functools.partial(kernel, shards, groups, docs), out_shape...]
    all_to_all x3 -> x0, waiting for transfers between devices: 65.4 us -> none  [the longest x1 33.5 us: body(): lax.all_to_all(grad_q, 'head', split_axis=0, concat_axis=1, tiled=True)]
    all_gather x2 -> x0, waiting for transfers between devices: 57.8 us -> none  [the longest x1 35.1 us: body(): lax.all_gather(summary_bwd[None], 'seq', axis=0, tiled=True)]
    dot_general x10 -> x0, matrix products: 57.5 us -> none  [the longest x1 15.5 us: body(): jnp.einsum('ih,ihde->hde', mixing_fwd, gathered_fwd, precision=lax.Precis...]
    all_to_all x6 -> x0, local copies, waits for them, and re-layouts: 24.4 us -> none  [the longest x2 8.25 us: body(): lax.all_to_all(grad_v, 'head', split_axis=0, concat_axis=1, tiled=True)]
    all_to_all x3 -> x0, starting transfers between devices: 13.7 us -> none  [the longest x1 4.62 us: body(): lax.all_to_all(grad_v, 'head', split_axis=0, concat_axis=1, tiled=True)]
    unnamed x15 -> x9, local copies, waits for them, and re-layouts: 15.5 us -> 6.29 us
    convert_element_type x3 -> x0, local copies, waits for them, and re-layouts: 8.01 us -> none  [the longest x1 2.67 us: body(): (local_v + outer_v).astype(jnp.bfloat16)]
  transfers between devices with their start and end apart: 5 -> 0, of which waited for: 4 -> 0; matrix products, arithmetic and copies ran while one was open for 32% -> 0% of each run, Pallas kernels for 0% -> 0%
where the time goes in v1:
time: 157 us; the launch traced here: 156 us
  Pallas kernels  149 us (95%)
  local copies, waits for them, and re-layouts  6.29 us (4%)
    pallas_call x1, Pallas kernels, body(): pl.pallas_call(functools.partial(kernel, shards, groups, docs), out_shape...  149 us
    unnamed x9, local copies, waits for them, and re-layouts  6.29 us

profile of v1, /device:TPU:0, one launch (start us, length us, event | category | flops | bytes accessed | tf_op | source)
XLA Modules:
  0.0 155.7 jit_solution(6940033473281485018)
XLA Ops:
  0.6 0.0 copy-start
  0.6 0.6 copy-done
  1.3 0.0 copy-start.1
  1.3 0.7 copy-done.1
  1.9 148.8 %shard_map.85 = (bf16[128,8192]{1,0:T(8,128)(2,1)S(1)}, bf16[128,8192]{1,0:T(8,128)(2,1)S(1)}, bf16[128,8192]{1,0:T(8,128)(2,1)}) custom-call(s32[8]{0:T(128)S(1)} %copy-done, f32[16]{0:T(128)S(1)} %copy-done.1, bf16[512,2048]{1,0:T(8,128)(2,1)} %q_hbm.1, bf16[512,2048]{1,0:T(8,128)(2,1)} %k_hbm.1, bf16[512,2048]{1,0:T(8,128)(2,1)} %v_hbm.1, ...), custom_call_target="tpu_custom_call" | custom-call | flops 6710886400 | bytes 14680064 | tf_op jit(solution)/shard_map/pallas_call | solution.py:264
  150.7 1.3 copy.12
  152.1 0.0 copy-start.2
  152.1 1.3 copy.13
  153.4 1.0 copy-done.2
  154.4 1.3 copy.14
Async XLA Ops:
  0.6 0.7 copy-start
  1.3 0.7 copy-start.1
  152.1 2.3 %copy-start.2 = (bf16[128,8192]{1,0:T(8,128)(2,1)S(1)}, bf16[128,8192]{1,0:T(8,128)(2,1)}, u32[]{:S(2)}) copy-start(bf16[128,8192]{1,0:T(8,128)(2,1)} %get-tuple-element.8) | copy-start | bytes 6291460

commit v2 on v1

--- a/solution.py
+++ b/solution.py
@@ -10,6 +10,7 @@
 MESH = pl.DeviceIdType.MESH
 NEVER = 1e30
 LEAD = 3
+VMEM_BYTES = 62 * 1024 * 1024
 
 
 def dot(a, b, dims):
@@ -25,15 +26,15 @@
     shards,
     groups,
     docs,
-    lengths,
-    rates,
+    lengths_hbm,
+    rates_hbm,
     q_hbm,
     k_hbm,
     v_hbm,
     g_hbm,
-    dq_hbm,
-    dk_hbm,
-    dv_hbm,
+    land,
+    lengths,
+    rates,
     rows_in,
     dist,
     row_dist,
@@ -41,21 +42,19 @@
     gathered,
     acc,
     stage,
-    land,
     gaps,
     load_sem,
     sum_send,
     sum_recv,
     out_send,
     out_recv,
-    write_sem,
+    small_sem,
 ):
     heads, _, length, head_dim = rows_in.shape
     part = length // groups
     shard = lax.axis_index("seq")
     group = lax.axis_index("head")
     inputs = (q_hbm, k_hbm, v_hbm, g_hbm)
-    outputs = (dq_hbm, dk_hbm, dv_hbm)
 
     def load(h):
         columns = pl.ds(pl.multiple_of(h * head_dim, head_dim), head_dim)
@@ -64,10 +63,12 @@
             for i, ref in enumerate(inputs)
         ]
 
-    @pl.loop(0, heads)
-    def _(h):
-        for copy in load(h):
-            copy.start()
+    small = [
+        pltpu.make_async_copy(lengths_hbm, lengths, small_sem.at[0]),
+        pltpu.make_async_copy(rates_hbm, rates, small_sem.at[1]),
+    ]
+    for copy in small + load(0):
+        copy.start()
 
     barrier = pltpu.get_barrier_semaphore()
     for d in range(1, shards):
@@ -78,6 +79,8 @@
         pl.semaphore_signal(barrier, inc=1, device_id=(shard, peer), device_id_type=MESH)
 
     first = shard * length
+    for copy in small:
+        copy.wait()
 
     def starts():
         total = jnp.int32(0)
@@ -101,8 +104,6 @@
     where = offset.astype(jnp.float32)
     row_dist[0] = jnp.where(segment == seg_last, length - 1.0 - where, NEVER)
     row_dist[1] = jnp.where(segment == seg_first, where, NEVER)
-    row_dist[2] = jnp.where(segment == seg_prev, where + 1.0, NEVER)
-    row_dist[3] = jnp.where(segment == seg_next, length - where, NEVER)
 
     def summarise(h):
         pltpu.make_async_copy(rows_in.at[h], rows_in.at[h], load_sem.at[h]).wait()
@@ -133,6 +134,14 @@
     pl.semaphore_wait(barrier, shards + groups - 2)
     send_sums(0)
 
+    @pl.loop(1, heads)
+    def _(h):
+        for copy in load(h):
+            copy.start()
+
+    row_dist[2] = jnp.where(segment == seg_prev, where + 1.0, NEVER)
+    row_dist[3] = jnp.where(segment == seg_next, length - where, NEVER)
+
     for d in range(1, shards):
         source = lax.rem(shard - d + shards, shards)
         ahead = (shard + shards - d) // shards
@@ -164,18 +173,14 @@
 
     order = sorted(range(1, groups), key=lambda d: abs(2 * d - groups))
 
-    def own(h):
-        columns = pl.ds(pl.multiple_of((group * heads + h) * head_dim, head_dim), head_dim)
-        return [
-            pltpu.make_async_copy(stage.at[h, group, c], ref.at[:, columns], write_sem)
-            for c, ref in enumerate(outputs)
-        ]
+    def columns_of(source, h):
+        return pl.ds(pl.multiple_of((source * heads + h) * head_dim, head_dim), head_dim)
 
     def push(h, d):
         peer = lax.rem(group + d, groups)
         return pltpu.make_async_remote_copy(
             src_ref=stage.at[h, peer],
-            dst_ref=land.at[d - 1, h],
+            dst_ref=land.at[:, :, columns_of(group, h)],
             send_sem=out_send,
             recv_sem=out_recv.at[d - 1, h],
             device_id=(shard, peer),
@@ -223,30 +228,38 @@
             stage[h, :, c] = total.astype(jnp.bfloat16).reshape(groups, part, head_dim)
         for d in order:
             push(h, d).start()
-        for copy in own(h):
-            copy.start()
-
-    def landed(h, d):
-        source = lax.rem(group - d + groups, groups)
-        columns = pl.ds(pl.multiple_of((source * heads + h) * head_dim, head_dim), head_dim)
-        return [
-            pltpu.make_async_copy(land.at[d - 1, h, c], ref.at[:, columns], write_sem)
-            for c, ref in enumerate(outputs)
-        ]
+        land[:, :, columns_of(group, h)] = stage[h, group]
 
     @pl.loop(0, heads)
     def _(h):
         for d in order:
             push(h, d).wait_recv()
-            for copy in landed(h, d):
-                copy.start()
 
     @pl.loop(0, heads)
     def _(h):
         pltpu.make_async_copy(gathered.at[h], gathered.at[h], sum_send.at[h]).wait()
 
-    pltpu.make_async_copy(land, land, out_send).wait()
-    pltpu.make_async_copy(stage, stage, write_sem).wait()
+    sent = stage.at[:, pl.ds(0, groups - 1)]
+    pltpu.make_async_copy(sent, sent, out_send).wait()
+
+
+def write_out(land, dq_hbm, dk_hbm, dv_hbm, write_sem):
+    columns = land.shape[2]
+    pieces = 4
+    width = columns // pieces
+    copies = []
+    for c, ref in enumerate((dq_hbm, dk_hbm, dv_hbm)):
+        for i in range(pieces):
+            piece = pl.ds(i * width, width)
+            copies.append(
+                pltpu.make_async_copy(
+                    land.at[c, :, piece], ref.at[:, piece], write_sem.at[c * pieces + i]
+                )
+            )
+    for copy in copies:
+        copy.start()
+    for copy in copies:
+        copy.wait()
 
 
 def body(queries, keys, values, grad_out, rates, doc_lengths):
@@ -257,16 +270,17 @@
     groups = lax.axis_size("head")
     part = length // groups
     docs = doc_lengths.shape[0]
-    smem = pl.BlockSpec(memory_space=pltpu.SMEM)
-    hbm = pl.BlockSpec(memory_space=pl.ANY)
+    hbm = pl.BlockSpec(memory_space=pltpu.HBM)
+    vmem = pl.BlockSpec(memory_space=pltpu.VMEM)
     bf16, f32 = jnp.bfloat16, jnp.float32
-    out = jax.ShapeDtypeStruct((part, groups * columns), bf16)
-    return pl.pallas_call(
+    landed = pl.pallas_call(
         functools.partial(kernel, shards, groups, docs),
-        out_shape=(out, out, out),
-        in_specs=[smem, smem, hbm, hbm, hbm, hbm],
-        out_specs=(hbm, hbm, hbm),
+        out_shape=pltpu.VMEM((3, part, groups * columns), bf16),
+        in_specs=[hbm] * 6,
+        out_specs=vmem,
         scratch_shapes=[
+            pltpu.SMEM(doc_lengths.shape, jnp.int32),
+            pltpu.SMEM(rates.shape, f32),
             pltpu.VMEM((heads, 4, length, head_dim), bf16),
             pltpu.VMEM((length, length), f32),
             pltpu.VMEM((4, length, head_dim), f32),
@@ -274,17 +288,16 @@
             pltpu.VMEM((heads, shards - 1, head_dim, head_dim), f32),
             pltpu.VMEM((3, length, head_dim), f32),
             pltpu.VMEM((heads, groups, 3, part, head_dim), bf16),
-            pltpu.VMEM((groups - 1, heads, 3, part, head_dim), bf16),
             pltpu.SMEM((2, shards - 1), f32),
             pltpu.SemaphoreType.DMA((heads,)),
             pltpu.SemaphoreType.DMA((heads,)),
             pltpu.SemaphoreType.DMA((heads,)),
             pltpu.SemaphoreType.DMA,
             pltpu.SemaphoreType.DMA((groups - 1, heads)),
-            pltpu.SemaphoreType.DMA,
+            pltpu.SemaphoreType.DMA((2,)),
         ],
         compiler_params=pltpu.CompilerParams(
-            collective_id=0, has_side_effects=True, vmem_limit_bytes=48 * 1024 * 1024
+            collective_id=0, has_side_effects=True, vmem_limit_bytes=VMEM_BYTES - 6 * part * groups * columns
         ),
         cost_estimate=pl.CostEstimate(
             flops=heads * length * (10 * length + 10 * head_dim) * head_dim,
@@ -292,6 +305,14 @@
             transcendentals=heads * length * (length + 4 * head_dim),
         ),
     )(doc_lengths, rates, queries, keys, values, grad_out)
+    out = jax.ShapeDtypeStruct((part, groups * columns), bf16)
+    return pl.pallas_call(
+        write_out,
+        out_shape=(out, out, out),
+        in_specs=[vmem],
+        out_specs=(hbm, hbm, hbm),
+        scratch_shapes=[pltpu.SemaphoreType.DMA((12,))],
+    )(landed)
 
 
 def solution(mesh):

time: 157 us -> 158 us (level)
  Pallas kernels: 149 us -> 153 us
  local copies, waits for them, and re-layouts: 6.29 us -> 2.65 us
    pallas_call x0 -> x1, Pallas kernels: none -> 5.53 us  [body(): pl.pallas_call(write_out, out_shape=(out, out, out), in_specs=[vmem], out...]
    unnamed x9 -> x2, local copies, waits for them, and re-layouts: 6.29 us -> 2.65 us
where the time goes in v2:
time: 158 us; the launch traced here: 156 us
  Pallas kernels  153 us (97%)
  local copies, waits for them, and re-layouts  2.65 us (2%)
    pallas_call x1, Pallas kernels, body(): pl.pallas_call(functools.partial(kernel, shards, groups, docs), out_shape...  147 us
    pallas_call x1, Pallas kernels, body(): pl.pallas_call(write_out, out_shape=(out, out, out), in_specs=[vmem], out...  5.53 us

profile of v2, /device:TPU:0, one launch (start us, length us, event | category | flops | bytes accessed | tf_op | source)
XLA Modules:
  0.0 156.3 jit_solution(10773964323372743749)
XLA Ops:
  0.6 147.4 %shard_map.85.land = bf16[3,128,8192]{2,1,0:T(8,128)(2,1)S(1)} custom-call(s32[8]{0:T(128)} %lengths_hbm.1, f32[16]{0:T(128)} %rates_hbm.1, bf16[512,2048]{1,0:T(8,128)(2,1)} %q_hbm.1, bf16[512,2048]{1,0:T(8,128)(2,1)} %k_hbm.1, bf16[512,2048]{1,0:T(8,128)(2,1)} %v_hbm.1, bf16[512,2048]{1,0:T(8,128)(2,1)} %g_hbm.1), custom_call_target="tpu_custom_call" | custom-call | flops 6710886400 | bytes 14680064 | tf_op jit(solution)/shard_map/pallas_call | solution.py:276
  148.1 0.0 copy-start
  148.1 2.6 %copy-done = bf16[3,128,8192]{2,1,0:T(8,128)(2,1)} copy-done((bf16[3,128,8192]{2,1,0:T(8,128)(2,1)}, bf16[3,128,8192]{2,1,0:T(8,128)(2,1)S(1)}, u32[]{:S(2)}) %copy-start) | copy-done | bytes 6291480
  150.7 5.5 %shard_map.86 = (bf16[128,8192]{1,0:T(8,128)(2,1)}, bf16[128,8192]{1,0:T(8,128)(2,1)}, bf16[128,8192]{1,0:T(8,128)(2,1)}) custom-call(bf16[3,128,8192]{2,1,0:T(8,128)(2,1)} %copy-done), custom_call_target="tpu_custom_call" | custom-call | tf_op jit(solution)/shard_map/pallas_call | solution.py:309
Async XLA Ops:
  148.1 2.7 %copy-start = (bf16[3,128,8192]{2,1,0:T(8,128)(2,1)}, bf16[3,128,8192]{2,1,0:T(8,128)(2,1)S(1)}, u32[]{:S(2)}) copy-start(bf16[3,128,8192]{2,1,0:T(8,128)(2,1)S(1)} %shard_map.85.land) | copy-start | bytes 18874372

commit v3 on v2

--- a/solution.py
+++ b/solution.py
@@ -9,7 +9,6 @@
 
 MESH = pl.DeviceIdType.MESH
 NEVER = 1e30
-LEAD = 3
 VMEM_BYTES = 62 * 1024 * 1024
 
 
@@ -39,11 +38,15 @@
     dist,
     row_dist,
     sums,
+    mates,
+    pair_sums,
     gathered,
     acc,
     stage,
     gaps,
     load_sem,
+    mate_send,
+    mate_recv,
     sum_send,
     sum_recv,
     out_send,
@@ -54,6 +57,7 @@
     part = length // groups
     shard = lax.axis_index("seq")
     group = lax.axis_index("head")
+    pairs, pair, core = shards // 2, shard // 2, lax.rem(shard, 2)
     inputs = (q_hbm, k_hbm, v_hbm, g_hbm)
 
     def load(h):
@@ -111,53 +115,93 @@
         weighted_k = (
             rows_in[h, 1].astype(jnp.float32) * jnp.exp(-rate * row_dist[0])
         ).astype(jnp.bfloat16)
-        sums[0, h] = dot(weighted_k, rows_in[h, 2], TN)
+        sums[h, 0] = dot(weighted_k, rows_in[h, 2], TN)
         weighted_q = (
             rows_in[h, 0].astype(jnp.float32) * jnp.exp(-rate * row_dist[1])
         ).astype(jnp.bfloat16)
-        sums[1, h] = dot(weighted_q, rows_in[h, 3], TN)
+        sums[h, 1] = dot(weighted_q, rows_in[h, 3], TN)
+
+    def swap(h):
+        return pltpu.make_async_remote_copy(
+            src_ref=sums.at[h],
+            dst_ref=mates.at[h],
+            send_sem=mate_send,
+            recv_sem=mate_recv.at[h],
+            device_id=(pair * 2 + 1 - core, group),
+            device_id_type=MESH,
+        )
+
+    def factor(way, entry, rate):
+        return jnp.exp(jnp.full((1, head_dim), -rate * gaps[way, entry]))
 
     def send_sums(h):
-        for d in range(1, shards):
-            peer = lax.rem(shard + d, shards)
-            back = (shard + d) // shards
-            pltpu.make_async_remote_copy(
-                src_ref=sums.at[back, h],
-                dst_ref=gathered.at[h, d - 1],
-                send_sem=sum_send.at[h],
-                recv_sem=sum_recv.at[h],
-                device_id=(peer, group),
-                device_id_type=MESH,
-            ).start()
-
+        swap(h).wait_recv()
+        rate = rates[h]
+        half = pl.ds(pl.multiple_of(core * (head_dim // 2), head_dim // 2), head_dim // 2)
+        for way in range(2):
+            pair_sums[h, way] = (
+                factor(way, pairs, rate) * sums[h, way, half]
+                + factor(way, pairs + 1, rate) * mates[h, way, half]
+            )
+        for d in range(1, pairs):
+            peer = lax.rem(pair + d, pairs)
+            back = (pair + d) // pairs
+            for side in range(2):
+                pltpu.make_async_remote_copy(
+                    src_ref=pair_sums.at[h, back],
+                    dst_ref=gathered.at[h, d - 1, core],
+                    send_sem=sum_send,
+                    recv_sem=sum_recv.at[h],
+                    device_id=(peer * 2 + side, group),
+                    device_id_type=MESH,
+                ).start()
+
+    lead = min(3, heads)
     summarise(0)
     pl.semaphore_wait(barrier, shards + groups - 2)
-    send_sums(0)
-
-    @pl.loop(1, heads)
+    swap(0).start()
+    for h in range(1, lead):
+        for copy in load(h):
+            copy.start()
+
+    for d in range(1, pairs):
+        source = lax.rem(pair - d + pairs, pairs)
+        ahead = (pair + pairs - d) // pairs
+        same_fwd = seg((source + 1) * 2 * length - 1) == seg_prev
+        same_bwd = seg(source * 2 * length) == seg_next
+        gap_fwd = (2 * (d - 1) + core) * length
+        gap_bwd = (2 * (pairs - d) - 1 - core) * length
+        gaps[0, d - 1] = jnp.where(
+            jnp.logical_and(ahead == 1, same_fwd), gap_fwd.astype(jnp.float32), NEVER
+        )
+        gaps[1, d - 1] = jnp.where(
+            jnp.logical_and(ahead == 0, same_bwd), gap_bwd.astype(jnp.float32), NEVER
+        )
+    left = pair * 2 * length
+    kept_fwd = seg(left + 2 * length - 1) == seg(left + length - 1)
+    kept_bwd = seg(left) == seg(left + length)
+    step_fwd = jnp.where(kept_fwd, float(length), NEVER)
+    step_bwd = jnp.where(kept_bwd, float(length), NEVER)
+    is_left = core == 0
+    gaps[0, pairs - 1] = jnp.where(is_left, NEVER, 0.0)
+    gaps[1, pairs - 1] = jnp.where(is_left, 0.0, NEVER)
+    gaps[0, pairs] = jnp.where(is_left, step_fwd, 0.0)
+    gaps[0, pairs + 1] = jnp.where(is_left, 0.0, step_fwd)
+    gaps[1, pairs] = jnp.where(is_left, 0.0, step_bwd)
+    gaps[1, pairs + 1] = jnp.where(is_left, step_bwd, 0.0)
+
+    for h in range(1, lead):
+        summarise(h)
+        swap(h).start()
+        send_sums(h - 1)
+
+    @pl.loop(lead, heads)
     def _(h):
         for copy in load(h):
             copy.start()
 
     row_dist[2] = jnp.where(segment == seg_prev, where + 1.0, NEVER)
     row_dist[3] = jnp.where(segment == seg_next, length - where, NEVER)
-
-    for d in range(1, shards):
-        source = lax.rem(shard - d + shards, shards)
-        ahead = (shard + shards - d) // shards
-        same_fwd = seg((source + 1) * length - 1) == seg_prev
-        same_bwd = seg(source * length) == seg_next
-        gaps[0, d - 1] = jnp.where(
-            jnp.logical_and(ahead == 1, same_fwd), float(length * (d - 1)), NEVER
-        )
-        gaps[1, d - 1] = jnp.where(
-            jnp.logical_and(ahead == 0, same_bwd), float(length * (shards - d - 1)), NEVER
-        )
-
-    lead = min(LEAD, heads)
-    for h in range(1, lead):
-        summarise(h)
-        send_sums(h)
 
     tile = min(256, length)
     tiles = length // tile
@@ -192,7 +236,11 @@
         @pl.when(h + lead < heads)
         def _():
             summarise(h + lead)
-            send_sums(h + lead)
+            swap(h + lead).start()
+
+        @pl.when(h + lead - 1 < heads)
+        def _():
+            send_sums(h + lead - 1)
 
         rate = rates[h]
         for i in range(tiles):
@@ -211,12 +259,12 @@
             acc[2, rows] = dv[i * tile :]
 
         pltpu.make_async_copy(gathered.at[h], gathered.at[h], sum_recv.at[h]).wait()
-        state = jnp.zeros((head_dim, head_dim), jnp.float32)
-        back = jnp.zeros((head_dim, head_dim), jnp.float32)
-        for d in range(shards - 1):
-            summary = gathered[h, d]
-            state += jnp.exp(jnp.full((1, head_dim), -rate * gaps[0, d])) * summary
-            back += jnp.exp(jnp.full((1, head_dim), -rate * gaps[1, d])) * summary
+        state = factor(0, pairs - 1, rate) * mates[h, 0]
+        back = factor(1, pairs - 1, rate) * mates[h, 1]
+        for d in range(pairs - 1):
+            summary = gathered[h, d].reshape(head_dim, head_dim)
+            state += factor(0, d, rate) * summary
+            back += factor(1, d, rate) * summary
         state = state.astype(jnp.bfloat16)
         back = back.astype(jnp.bfloat16)
         factor_in = jnp.exp(-rate * row_dist[2])
@@ -235,10 +283,8 @@
         for d in order:
             push(h, d).wait_recv()
 
-    @pl.loop(0, heads)
-    def _(h):
-        pltpu.make_async_copy(gathered.at[h], gathered.at[h], sum_send.at[h]).wait()
-
+    pltpu.make_async_copy(sums, sums, mate_send).wait()
+    pltpu.make_async_copy(gathered, gathered, sum_send).wait()
     sent = stage.at[:, pl.ds(0, groups - 1)]
     pltpu.make_async_copy(sent, sent, out_send).wait()
 
@@ -284,13 +330,17 @@
             pltpu.VMEM((heads, 4, length, head_dim), bf16),
             pltpu.VMEM((length, length), f32),
             pltpu.VMEM((4, length, head_dim), f32),
-            pltpu.VMEM((2, heads, head_dim, head_dim), f32),
-            pltpu.VMEM((heads, shards - 1, head_dim, head_dim), f32),
+            pltpu.VMEM((heads, 2, head_dim, head_dim), f32),
+            pltpu.VMEM((heads, 2, head_dim, head_dim), f32),
+            pltpu.VMEM((heads, 2, head_dim // 2, head_dim), f32),
+            pltpu.VMEM((heads, shards // 2 - 1, 2, head_dim // 2, head_dim), f32),
             pltpu.VMEM((3, length, head_dim), f32),
             pltpu.VMEM((heads, groups, 3, part, head_dim), bf16),
-            pltpu.SMEM((2, shards - 1), f32),
+            pltpu.SMEM((2, shards // 2 + 2), f32),
             pltpu.SemaphoreType.DMA((heads,)),
+            pltpu.SemaphoreType.DMA,
             pltpu.SemaphoreType.DMA((heads,)),
+            pltpu.SemaphoreType.DMA,
             pltpu.SemaphoreType.DMA((heads,)),
             pltpu.SemaphoreType.DMA,
             pltpu.SemaphoreType.DMA((groups - 1, heads)),
@@ -309,9 +359,10 @@
     return pl.pallas_call(
         write_out,
         out_shape=(out, out, out),
-        in_specs=[vmem],
+        in_specs=[pl.BlockSpec(memory_space=pl.ANY)],
         out_specs=(hbm, hbm, hbm),
         scratch_shapes=[pltpu.SemaphoreType.DMA((12,))],
+        compiler_params=pltpu.CompilerParams(vmem_limit_bytes=1024 * 1024),
     )(landed)
 
 

time: 158 us -> 151 us (0.956); the launches traced: 156 us -> 151 us
  Pallas kernels: 153 us -> 150 us
  local copies, waits for them, and re-layouts: 2.65 us -> 0 us
    pallas_call x1, Pallas kernels: 5.53 us -> 2.75 us  [body(): pl.pallas_call(write_out, out_shape=(out, out, out), in_specs=[pl.BlockSp...]
    unnamed x2 -> x0, local copies, waits for them, and re-layouts: 2.65 us -> none
where the time goes in v3:
time: 151 us
  Pallas kernels  150 us (99%)
    pallas_call x1, Pallas kernels, body(): pl.pallas_call(functools.partial(kernel, shards, groups, docs), out_shape...  147 us

profile of v3, /device:TPU:0, one launch (start us, length us, event | category | flops | bytes accessed | tf_op | source)
XLA Modules:
  0.0 150.9 jit_solution(8018831812930250467)
XLA Ops:
  0.6 147.5 %shard_map.85.land = bf16[3,128,8192]{2,1,0:T(8,128)(2,1)S(1)} custom-call(s32[8]{0:T(128)} %lengths_hbm.1, f32[16]{0:T(128)} %rates_hbm.1, bf16[512,2048]{1,0:T(8,128)(2,1)} %q_hbm.1, bf16[512,2048]{1,0:T(8,128)(2,1)} %k_hbm.1, bf16[512,2048]{1,0:T(8,128)(2,1)} %v_hbm.1, bf16[512,2048]{1,0:T(8,128)(2,1)} %g_hbm.1), custom_call_target="tpu_custom_call" | custom-call | flops 6710886400 | bytes 14680064 | tf_op jit(solution)/shard_map/pallas_call | solution.py:322
  148.1 2.8 %shard_map.86 = (bf16[128,8192]{1,0:T(8,128)(2,1)}, bf16[128,8192]{1,0:T(8,128)(2,1)}, bf16[128,8192]{1,0:T(8,128)(2,1)}) custom-call(bf16[3,128,8192]{2,1,0:T(8,128)(2,1)S(1)} %shard_map.85.land), custom_call_target="tpu_custom_call" | custom-call | tf_op jit(solution)/shard_map/pallas_call | solution.py:359

commit v4 on v3

--- a/solution.py
+++ b/solution.py
@@ -71,7 +71,7 @@
         pltpu.make_async_copy(lengths_hbm, lengths, small_sem.at[0]),
         pltpu.make_async_copy(rates_hbm, rates, small_sem.at[1]),
     ]
-    for copy in small + load(0):
+    for copy in small + load(0) + load(1):
         copy.start()
 
     barrier = pltpu.get_barrier_semaphore()
@@ -156,13 +156,22 @@
                     device_id_type=MESH,
                 ).start()
 
-    lead = min(3, heads)
     summarise(0)
-    pl.semaphore_wait(barrier, shards + groups - 2)
-    swap(0).start()
-    for h in range(1, lead):
-        for copy in load(h):
-            copy.start()
+
+    row_dist[2] = jnp.where(segment == seg_prev, where + 1.0, NEVER)
+    row_dist[3] = jnp.where(segment == seg_next, length - where, NEVER)
+
+    tile = min(256, length)
+    tiles = length // tile
+    across = lax.broadcasted_iota(jnp.int32, (1, length), 1)
+    seg_across = seg(first + across)
+    for i in range(tiles):
+        down = i * tile + lax.broadcasted_iota(jnp.int32, (tile, 1), 0)
+        seg_down = seg(first + down)
+        gap = down - across
+        dist[pl.ds(i * tile, tile), :] = jnp.where(
+            jnp.logical_and(seg_down == seg_across, gap >= 0), gap.astype(jnp.float32), NEVER
+        )
 
     for d in range(1, pairs):
         source = lax.rem(pair - d + pairs, pairs)
@@ -190,30 +199,11 @@
     gaps[1, pairs] = jnp.where(is_left, 0.0, step_bwd)
     gaps[1, pairs + 1] = jnp.where(is_left, step_bwd, 0.0)
 
-    for h in range(1, lead):
-        summarise(h)
-        swap(h).start()
-        send_sums(h - 1)
-
-    @pl.loop(lead, heads)
-    def _(h):
-        for copy in load(h):
-            copy.start()
-
-    row_dist[2] = jnp.where(segment == seg_prev, where + 1.0, NEVER)
-    row_dist[3] = jnp.where(segment == seg_next, length - where, NEVER)
-
-    tile = min(256, length)
-    tiles = length // tile
-    across = lax.broadcasted_iota(jnp.int32, (1, length), 1)
-    seg_across = seg(first + across)
-    for i in range(tiles):
-        down = i * tile + lax.broadcasted_iota(jnp.int32, (tile, 1), 0)
-        seg_down = seg(first + down)
-        gap = down - across
-        dist[pl.ds(i * tile, tile), :] = jnp.where(
-            jnp.logical_and(seg_down == seg_across, gap >= 0), gap.astype(jnp.float32), NEVER
-        )
+    pl.semaphore_wait(barrier, shards + groups - 2)
+    swap(0).start()
+    summarise(1)
+    swap(1).start()
+    send_sums(0)
 
     order = sorted(range(1, groups), key=lambda d: abs(2 * d - groups))
 
@@ -233,14 +223,10 @@
 
     @pl.loop(0, heads)
     def _(h):
-        @pl.when(h + lead < heads)
+        @pl.when(h + 2 < heads)
         def _():
-            summarise(h + lead)
-            swap(h + lead).start()
-
-        @pl.when(h + lead - 1 < heads)
-        def _():
-            send_sums(h + lead - 1)
+            for copy in load(h + 2):
+                copy.start()
 
         rate = rates[h]
         for i in range(tiles):
@@ -257,6 +243,15 @@
                 acc[2, pl.ds(0, i * tile)] += dv[: i * tile]
             acc[1, rows] = dk[i * tile :]
             acc[2, rows] = dv[i * tile :]
+
+        @pl.when(h + 1 < heads)
+        def _():
+            send_sums(h + 1)
+
+        @pl.when(h + 2 < heads)
+        def _():
+            summarise(h + 2)
+            swap(h + 2).start()
 
         pltpu.make_async_copy(gathered.at[h], gathered.at[h], sum_recv.at[h]).wait()
         state = factor(0, pairs - 1, rate) * mates[h, 0]

time: 151 us -> 151 us (level)
  no operation moved by 1% of the time
where the time goes in v4:
time: 151 us
  Pallas kernels  150 us (99%)
    pallas_call x1, Pallas kernels, body(): pl.pallas_call(functools.partial(kernel, shards, groups, docs), out_shape...  147 us

profile of v4, /device:TPU:0, one launch (start us, length us, event | category | flops | bytes accessed | tf_op | source)
XLA Modules:
  0.0 150.8 jit_solution(8755908887569181166)
XLA Ops:
  0.6 147.4 %shard_map.85.land = bf16[3,128,8192]{2,1,0:T(8,128)(2,1)S(1)} custom-call(s32[8]{0:T(128)} %lengths_hbm.1, f32[16]{0:T(128)} %rates_hbm.1, bf16[512,2048]{1,0:T(8,128)(2,1)} %q_hbm.1, bf16[512,2048]{1,0:T(8,128)(2,1)} %k_hbm.1, bf16[512,2048]{1,0:T(8,128)(2,1)} %v_hbm.1, bf16[512,2048]{1,0:T(8,128)(2,1)} %g_hbm.1), custom_call_target="tpu_custom_call" | custom-call | flops 6710886400 | bytes 14680064 | tf_op jit(solution)/shard_map/pallas_call | solution.py:317
  148.1 2.8 %shard_map.86 = (bf16[128,8192]{1,0:T(8,128)(2,1)}, bf16[128,8192]{1,0:T(8,128)(2,1)}, bf16[128,8192]{1,0:T(8,128)(2,1)}) custom-call(bf16[3,128,8192]{2,1,0:T(8,128)(2,1)S(1)} %shard_map.85.land), custom_call_target="tpu_custom_call" | custom-call | tf_op jit(solution)/shard_map/pallas_call | solution.py:354

commit v5 on v4

--- a/solution.py
+++ b/solution.py
@@ -36,6 +36,7 @@
     rates,
     rows_in,
     dist,
+    dist_t,
     row_dist,
     sums,
     mates,
@@ -172,6 +173,9 @@
         dist[pl.ds(i * tile, tile), :] = jnp.where(
             jnp.logical_and(seg_down == seg_across, gap >= 0), gap.astype(jnp.float32), NEVER
         )
+        dist_t[pl.ds(i * tile, tile), :] = jnp.where(
+            jnp.logical_and(seg_down == seg_across, gap <= 0), -gap.astype(jnp.float32), NEVER
+        )
 
     for d in range(1, pairs):
         source = lax.rem(pair - d + pairs, pairs)
@@ -207,6 +211,10 @@
 
     order = sorted(range(1, groups), key=lambda d: abs(2 * d - groups))
 
+    def crosses(d):
+        peer = lax.rem(group + d, groups)
+        return (2 * group < groups) != (2 * peer < groups)
+
     def columns_of(source, h):
         return pl.ds(pl.multiple_of((source * heads + h) * head_dim, head_dim), head_dim)
 
@@ -230,19 +238,17 @@
 
         rate = rates[h]
         for i in range(tiles):
-            rows, seen = pl.ds(i * tile, tile), (i + 1) * tile
-            q, g = rows_in[h, 0, rows], rows_in[h, 3, rows]
-            k, v = rows_in[h, 1, pl.ds(0, seen)], rows_in[h, 2, pl.ds(0, seen)]
-            decay = jnp.exp(-rate * dist[rows, pl.ds(0, seen)])
-            p = (decay * dot(g, v, NT)).astype(jnp.bfloat16)
-            a = (decay * dot(q, k, NT)).astype(jnp.bfloat16)
-            acc[0, rows] = dot(p, k, NN)
-            dk, dv = dot(p, q, TN), dot(a, g, TN)
-            if i:
-                acc[1, pl.ds(0, i * tile)] += dk[: i * tile]
-                acc[2, pl.ds(0, i * tile)] += dv[: i * tile]
-            acc[1, rows] = dk[i * tile :]
-            acc[2, rows] = dv[i * tile :]
+            rows = pl.ds(i * tile, tile)
+            seen = pl.ds(0, (i + 1) * tile)
+            later = pl.ds(i * tile, length - i * tile)
+            decay = jnp.exp(-rate * dist[rows, seen])
+            p = decay * dot(rows_in[h, 3, rows], rows_in[h, 2, seen], NT)
+            acc[0, rows] = dot(p.astype(jnp.bfloat16), rows_in[h, 1, seen], NN)
+            decay_t = jnp.exp(-rate * dist_t[rows, later])
+            p_t = decay_t * dot(rows_in[h, 2, rows], rows_in[h, 3, later], NT)
+            acc[1, rows] = dot(p_t.astype(jnp.bfloat16), rows_in[h, 0, later], NN)
+            a_t = decay_t * dot(rows_in[h, 1, rows], rows_in[h, 0, later], NT)
+            acc[2, rows] = dot(a_t.astype(jnp.bfloat16), rows_in[h, 3, later], NN)
 
         @pl.when(h + 1 < heads)
         def _():
@@ -269,8 +275,13 @@
         dv = acc[2] + dot(rows_in[h, 1], back, NN) * factor_back
         for c, total in enumerate((dq, dk, dv)):
             stage[h, :, c] = total.astype(jnp.bfloat16).reshape(groups, part, head_dim)
-        for d in order:
-            push(h, d).start()
+        for far in (True, False):
+            for d in order:
+
+                @pl.when(crosses(d) == far)
+                def _():
+                    push(h, d).start()
+
         land[:, :, columns_of(group, h)] = stage[h, group]
 
     @pl.loop(0, heads)
@@ -323,6 +334,7 @@
             pltpu.SMEM(doc_lengths.shape, jnp.int32),
             pltpu.SMEM(rates.shape, f32),
             pltpu.VMEM((heads, 4, length, head_dim), bf16),
+            pltpu.VMEM((length, length), f32),
             pltpu.VMEM((length, length), f32),
             pltpu.VMEM((4, length, head_dim), f32),
             pltpu.VMEM((heads, 2, head_dim, head_dim), f32),

time: 151 us -> 151 us (level)
  no operation moved by 1% of the time
where the time goes in v5:
time: 151 us
  Pallas kernels  150 us (99%)
    pallas_call x1, Pallas kernels, body(): pl.pallas_call(functools.partial(kernel, shards, groups, docs), out_shape...  148 us

profile of v5, /device:TPU:0, one launch (start us, length us, event | category | flops | bytes accessed | tf_op | source)
XLA Modules:
  0.0 151.0 jit_solution(2856953523289941449)
XLA Ops:
  0.6 147.6 %shard_map.85.land = bf16[3,128,8192]{2,1,0:T(8,128)(2,1)S(1)} custom-call(s32[8]{0:T(128)} %lengths_hbm.1, f32[16]{0:T(128)} %rates_hbm.1, bf16[512,2048]{1,0:T(8,128)(2,1)} %q_hbm.1, bf16[512,2048]{1,0:T(8,128)(2,1)} %k_hbm.1, bf16[512,2048]{1,0:T(8,128)(2,1)} %v_hbm.1, bf16[512,2048]{1,0:T(8,128)(2,1)} %g_hbm.1), custom_call_target="tpu_custom_call" | custom-call | flops 6710886400 | bytes 14680064 | tf_op jit(solution)/shard_map/pallas_call | solution.py:328
  148.2 2.8 %shard_map.86 = (bf16[128,8192]{1,0:T(8,128)(2,1)}, bf16[128,8192]{1,0:T(8,128)(2,1)}, bf16[128,8192]{1,0:T(8,128)(2,1)}) custom-call(bf16[3,128,8192]{2,1,0:T(8,128)(2,1)S(1)} %shard_map.85.land), custom_call_target="tpu_custom_call" | custom-call | tf_op jit(solution)/shard_map/pallas_call | solution.py:366

commit v6 on v5

--- a/solution.py
+++ b/solution.py
@@ -229,6 +229,17 @@
             device_id_type=MESH,
         )
 
+    def push_across(h):
+        for d in order:
+
+            @pl.when(crosses(d))
+            def _():
+                push(h, d).start()
+
+    inner = jnp.logical_and(group > 0, group < groups - 1)
+    end = jnp.where(2 * group < groups, 0, groups - 1)
+    from_end = lax.rem(group - end + groups, groups)
+
     @pl.loop(0, heads)
     def _(h):
         @pl.when(h + 2 < heads)
@@ -275,19 +286,39 @@
         dv = acc[2] + dot(rows_in[h, 1], back, NN) * factor_back
         for c, total in enumerate((dq, dk, dv)):
             stage[h, :, c] = total.astype(jnp.bfloat16).reshape(groups, part, head_dim)
-        for far in (True, False):
-            for d in order:
-
-                @pl.when(crosses(d) == far)
-                def _():
-                    push(h, d).start()
+        @pl.when(jnp.logical_not(inner))
+        def _():
+            push_across(h)
+
+        @pl.when(jnp.logical_and(inner, lax.rem(h, 4) == 0))
+        def _():
+            push_across(h // 4)
+
+        for d in order:
+
+            @pl.when(jnp.logical_not(crosses(d)))
+            def _():
+                push(h, d).start()
 
         land[:, :, columns_of(group, h)] = stage[h, group]
+
+    pushed = (heads + 3) // 4
+
+    @pl.when(inner)
+    def _():
+        @pl.loop(pushed, heads)
+        def _(h):
+            push(h - 1, from_end).wait_recv()
+            push_across(h)
 
     @pl.loop(0, heads)
     def _(h):
+        paced = jnp.logical_and(inner, jnp.logical_and(h >= pushed - 1, h < heads - 1))
         for d in order:
-            push(h, d).wait_recv()
+
+            @pl.when(jnp.logical_not(jnp.logical_and(paced, from_end == d)))
+            def _():
+                push(h, d).wait_recv()
 
     pltpu.make_async_copy(sums, sums, mate_send).wait()
     pltpu.make_async_copy(gathered, gathered, sum_send).wait()

time: 151 us -> 152 us (level)
  Pallas kernels: 150 us -> 152 us
where the time goes in v6:
time: 152 us
  Pallas kernels  152 us (100%)
    pallas_call x1, Pallas kernels, body(): pl.pallas_call(functools.partial(kernel, shards, groups, docs), out_shape...  149 us

profile of v6, /device:TPU:0, one launch (start us, length us, event | category | flops | bytes accessed | tf_op | source)
XLA Modules:
  0.0 152.2 jit_solution(6130300238835585657)
XLA Ops:
  0.6 148.8 %shard_map.85.land = bf16[3,128,8192]{2,1,0:T(8,128)(2,1)S(1)} custom-call(s32[8]{0:T(128)} %lengths_hbm.1, f32[16]{0:T(128)} %rates_hbm.1, bf16[512,2048]{1,0:T(8,128)(2,1)} %q_hbm.1, bf16[512,2048]{1,0:T(8,128)(2,1)} %k_hbm.1, bf16[512,2048]{1,0:T(8,128)(2,1)} %v_hbm.1, bf16[512,2048]{1,0:T(8,128)(2,1)} %g_hbm.1), custom_call_target="tpu_custom_call" | custom-call | flops 6710886400 | bytes 14680064 | tf_op jit(solution)/shard_map/pallas_call | solution.py:359
  149.4 2.8 %shard_map.86 = (bf16[128,8192]{1,0:T(8,128)(2,1)}, bf16[128,8192]{1,0:T(8,128)(2,1)}, bf16[128,8192]{1,0:T(8,128)(2,1)}) custom-call(bf16[3,128,8192]{2,1,0:T(8,128)(2,1)S(1)} %shard_map.85.land), custom_call_target="tpu_custom_call" | custom-call | tf_op jit(solution)/shard_map/pallas_call | solution.py:397

commit v7 on v5

--- a/solution.py
+++ b/solution.py
@@ -44,6 +44,7 @@
     gathered,
     acc,
     stage,
+    arrived,
     gaps,
     load_sem,
     mate_send,
@@ -211,10 +212,6 @@
 
     order = sorted(range(1, groups), key=lambda d: abs(2 * d - groups))
 
-    def crosses(d):
-        peer = lax.rem(group + d, groups)
-        return (2 * group < groups) != (2 * peer < groups)
-
     def columns_of(source, h):
         return pl.ds(pl.multiple_of((source * heads + h) * head_dim, head_dim), head_dim)
 
@@ -222,7 +219,7 @@
         peer = lax.rem(group + d, groups)
         return pltpu.make_async_remote_copy(
             src_ref=stage.at[h, peer],
-            dst_ref=land.at[:, :, columns_of(group, h)],
+            dst_ref=arrived.at[h, d - 1],
             send_sem=out_send,
             recv_sem=out_recv.at[d - 1, h],
             device_id=(shard, peer),
@@ -275,24 +272,20 @@
         dv = acc[2] + dot(rows_in[h, 1], back, NN) * factor_back
         for c, total in enumerate((dq, dk, dv)):
             stage[h, :, c] = total.astype(jnp.bfloat16).reshape(groups, part, head_dim)
-        for far in (True, False):
-            for d in order:
-
-                @pl.when(crosses(d) == far)
-                def _():
-                    push(h, d).start()
-
+        for d in order:
+            push(h, d).start()
         land[:, :, columns_of(group, h)] = stage[h, group]
 
     @pl.loop(0, heads)
     def _(h):
         for d in order:
             push(h, d).wait_recv()
+            source = lax.rem(group - d + groups, groups)
+            land[:, :, columns_of(source, h)] = arrived[h, d - 1]
 
     pltpu.make_async_copy(sums, sums, mate_send).wait()
     pltpu.make_async_copy(gathered, gathered, sum_send).wait()
-    sent = stage.at[:, pl.ds(0, groups - 1)]
-    pltpu.make_async_copy(sent, sent, out_send).wait()
+    pltpu.make_async_copy(arrived, arrived, out_send).wait()
 
 
 def write_out(land, dq_hbm, dk_hbm, dv_hbm, write_sem):
@@ -343,6 +336,7 @@
             pltpu.VMEM((heads, shards // 2 - 1, 2, head_dim // 2, head_dim), f32),
             pltpu.VMEM((3, length, head_dim), f32),
             pltpu.VMEM((heads, groups, 3, part, head_dim), bf16),
+            pltpu.VMEM((heads, groups - 1, 3, part, head_dim), bf16),
             pltpu.SMEM((2, shards // 2 + 2), f32),
             pltpu.SemaphoreType.DMA((heads,)),
             pltpu.SemaphoreType.DMA,

time: 151 us -> 151 us (level)
  no operation moved by 1% of the time
where the time goes in v7:
time: 151 us
  Pallas kernels  150 us (99%)
    pallas_call x1, Pallas kernels, body(): pl.pallas_call(functools.partial(kernel, shards, groups, docs), out_shape...  148 us

profile of v7, /device:TPU:0, one launch (start us, length us, event | category | flops | bytes accessed | tf_op | source)
XLA Modules:
  0.0 151.0 jit_solution(7959467442225591802)
XLA Ops:
  0.6 147.6 %shard_map.85.land = bf16[3,128,8192]{2,1,0:T(8,128)(2,1)S(1)} custom-call(s32[8]{0:T(128)} %lengths_hbm.1, f32[16]{0:T(128)} %rates_hbm.1, bf16[512,2048]{1,0:T(8,128)(2,1)} %q_hbm.1, bf16[512,2048]{1,0:T(8,128)(2,1)} %k_hbm.1, bf16[512,2048]{1,0:T(8,128)(2,1)} %v_hbm.1, bf16[512,2048]{1,0:T(8,128)(2,1)} %g_hbm.1), custom_call_target="tpu_custom_call" | custom-call | flops 6710886400 | bytes 14680064 | tf_op jit(solution)/shard_map/pallas_call | solution.py:321
  148.3 2.8 %shard_map.86 = (bf16[128,8192]{1,0:T(8,128)(2,1)}, bf16[128,8192]{1,0:T(8,128)(2,1)}, bf16[128,8192]{1,0:T(8,128)(2,1)}) custom-call(bf16[3,128,8192]{2,1,0:T(8,128)(2,1)S(1)} %shard_map.85.land), custom_call_target="tpu_custom_call" | custom-call | tf_op jit(solution)/shard_map/pallas_call | solution.py:360

commit v8 on v5

--- a/solution.py
+++ b/solution.py
@@ -68,20 +68,20 @@
             for i, ref in enumerate(inputs)
         ]
 
+    barrier = pltpu.get_barrier_semaphore()
+    for d in range(1, groups):
+        peer = lax.rem(group + d, groups)
+        pl.semaphore_signal(barrier, inc=1, device_id=(shard, peer), device_id_type=MESH)
+    for d in range(1, shards):
+        peer = lax.rem(shard + d, shards)
+        pl.semaphore_signal(barrier, inc=1, device_id=(peer, group), device_id_type=MESH)
+
     small = [
         pltpu.make_async_copy(lengths_hbm, lengths, small_sem.at[0]),
         pltpu.make_async_copy(rates_hbm, rates, small_sem.at[1]),
     ]
     for copy in small + load(0) + load(1):
         copy.start()
-
-    barrier = pltpu.get_barrier_semaphore()
-    for d in range(1, shards):
-        peer = lax.rem(shard + d, shards)
-        pl.semaphore_signal(barrier, inc=1, device_id=(peer, group), device_id_type=MESH)
-    for d in range(1, groups):
-        peer = lax.rem(group + d, groups)
-        pl.semaphore_signal(barrier, inc=1, device_id=(shard, peer), device_id_type=MESH)
 
     first = shard * length
     for copy in small:
@@ -211,18 +211,14 @@
 
     order = sorted(range(1, groups), key=lambda d: abs(2 * d - groups))
 
-    def crosses(d):
-        peer = lax.rem(group + d, groups)
-        return (2 * group < groups) != (2 * peer < groups)
-
     def columns_of(source, h):
         return pl.ds(pl.multiple_of((source * heads + h) * head_dim, head_dim), head_dim)
 
-    def push(h, d):
+    def push(h, d, which=pl.ds(0, 3)):
         peer = lax.rem(group + d, groups)
         return pltpu.make_async_remote_copy(
-            src_ref=stage.at[h, peer],
-            dst_ref=land.at[:, :, columns_of(group, h)],
+            src_ref=stage.at[h, peer, which],
+            dst_ref=land.at[which, :, columns_of(group, h)],
             send_sem=out_send,
             recv_sem=out_recv.at[d - 1, h],
             device_id=(shard, peer),
@@ -260,28 +256,24 @@
             swap(h + 2).start()
 
         pltpu.make_async_copy(gathered.at[h], gathered.at[h], sum_recv.at[h]).wait()
-        state = factor(0, pairs - 1, rate) * mates[h, 0]
-        back = factor(1, pairs - 1, rate) * mates[h, 1]
-        for d in range(pairs - 1):
-            summary = gathered[h, d].reshape(head_dim, head_dim)
-            state += factor(0, d, rate) * summary
-            back += factor(1, d, rate) * summary
-        state = state.astype(jnp.bfloat16)
-        back = back.astype(jnp.bfloat16)
-        factor_in = jnp.exp(-rate * row_dist[2])
+        def state_of(way):
+            total = factor(way, pairs - 1, rate) * mates[h, way]
+            for d in range(pairs - 1):
+                total += factor(way, d, rate) * gathered[h, d].reshape(head_dim, head_dim)
+            return total.astype(jnp.bfloat16)
+
+        def finish(c, outer):
+            total = (acc[c] + outer).astype(jnp.bfloat16)
+            stage[h, :, c] = total.reshape(groups, part, head_dim)
+            for d in order:
+                push(h, d, pl.ds(c, 1)).start()
+
+        state = state_of(0)
+        finish(0, dot(rows_in[h, 3], state, NT) * jnp.exp(-rate * row_dist[2]))
+        back = state_of(1)
         factor_back = jnp.exp(-rate * row_dist[3])
-        dq = acc[0] + dot(rows_in[h, 3], state, NT) * factor_in
-        dk = acc[1] + dot(rows_in[h, 2], back, NT) * factor_back
-        dv = acc[2] + dot(rows_in[h, 1], back, NN) * factor_back
-        for c, total in enumerate((dq, dk, dv)):
-            stage[h, :, c] = total.astype(jnp.bfloat16).reshape(groups, part, head_dim)
-        for far in (True, False):
-            for d in order:
-
-                @pl.when(crosses(d) == far)
-                def _():
-                    push(h, d).start()
-
+        finish(1, dot(rows_in[h, 2], back, NT) * factor_back)
+        finish(2, dot(rows_in[h, 1], back, NN) * factor_back)
         land[:, :, columns_of(group, h)] = stage[h, group]
 
     @pl.loop(0, heads)
@@ -296,16 +288,15 @@
 
 
 def write_out(land, dq_hbm, dk_hbm, dv_hbm, write_sem):
-    columns = land.shape[2]
-    pieces = 4
-    width = columns // pieces
+    rows = land.shape[1]
+    band = min(32, rows)
     copies = []
     for c, ref in enumerate((dq_hbm, dk_hbm, dv_hbm)):
-        for i in range(pieces):
-            piece = pl.ds(i * width, width)
+        for i in range(rows // band):
+            piece = pl.ds(i * band, band)
             copies.append(
                 pltpu.make_async_copy(
-                    land.at[c, :, piece], ref.at[:, piece], write_sem.at[c * pieces + i]
+                    land.at[c, piece], ref.at[piece], write_sem.at[c, i]
                 )
             )
     for copy in copies:
@@ -368,7 +359,7 @@
         out_shape=(out, out, out),
         in_specs=[pl.BlockSpec(memory_space=pl.ANY)],
         out_specs=(hbm, hbm, hbm),
-        scratch_shapes=[pltpu.SemaphoreType.DMA((12,))],
+        scratch_shapes=[pltpu.SemaphoreType.DMA((3, part // min(32, part)))],
         compiler_params=pltpu.CompilerParams(vmem_limit_bytes=1024 * 1024),
     )(landed)
 

time: 151 us -> 152 us (level)
  no operation moved by 1% of the time
where the time goes in v8:
time: 152 us
  Pallas kernels  151 us (99%)
    pallas_call x1, Pallas kernels, body(): pl.pallas_call(functools.partial(kernel, shards, groups, docs), out_shape...  149 us

profile of v8, /device:TPU:0, one launch (start us, length us, event | category | flops | bytes accessed | tf_op | source)
XLA Modules:
  0.0 152.1 jit_solution(18358429967398546507)
XLA Ops:
  0.6 148.7 %shard_map.85.land = bf16[3,128,8192]{2,1,0:T(8,128)(2,1)S(1)} custom-call(s32[8]{0:T(128)} %lengths_hbm.1, f32[16]{0:T(128)} %rates_hbm.1, bf16[512,2048]{1,0:T(8,128)(2,1)} %q_hbm.1, bf16[512,2048]{1,0:T(8,128)(2,1)} %k_hbm.1, bf16[512,2048]{1,0:T(8,128)(2,1)} %v_hbm.1, bf16[512,2048]{1,0:T(8,128)(2,1)} %g_hbm.1), custom_call_target="tpu_custom_call" | custom-call | flops 6710886400 | bytes 14680064 | tf_op jit(solution)/shard_map/pallas_call | solution.py:319
  149.4 2.8 %shard_map.86 = (bf16[128,8192]{1,0:T(8,128)(2,1)}, bf16[128,8192]{1,0:T(8,128)(2,1)}, bf16[128,8192]{1,0:T(8,128)(2,1)}) custom-call(bf16[3,128,8192]{2,1,0:T(8,128)(2,1)S(1)} %shard_map.85.land), custom_call_target="tpu_custom_call" | custom-call | tf_op jit(solution)/shard_map/pallas_call | solution.py:357

commit v9 on v4

--- a/solution.py
+++ b/solution.py
@@ -210,13 +210,18 @@
     def columns_of(source, h):
         return pl.ds(pl.multiple_of((source * heads + h) * head_dim, head_dim), head_dim)
 
-    def push(h, d):
+    bunch = stage.shape[-1] // head_dim
+    bunches = heads // bunch
+
+    def push(b, d):
         peer = lax.rem(group + d, groups)
         return pltpu.make_async_remote_copy(
-            src_ref=stage.at[h, peer],
-            dst_ref=land.at[:, :, columns_of(group, h)],
+            src_ref=stage.at[b, peer],
+            dst_ref=land.at[:, :, pl.ds(
+                pl.multiple_of((group * heads + b * bunch) * head_dim, head_dim), bunch * head_dim
+            )],
             send_sem=out_send,
-            recv_sem=out_recv.at[d - 1, h],
+            recv_sem=out_recv.at[d - 1, b],
             device_id=(shard, peer),
             device_id_type=MESH,
         )
@@ -267,16 +272,23 @@
         dq = acc[0] + dot(rows_in[h, 3], state, NT) * factor_in
         dk = acc[1] + dot(rows_in[h, 2], back, NT) * factor_back
         dv = acc[2] + dot(rows_in[h, 1], back, NN) * factor_back
+        inside = pl.ds(pl.multiple_of(lax.rem(h, bunch) * head_dim, head_dim), head_dim)
         for c, total in enumerate((dq, dk, dv)):
-            stage[h, :, c] = total.astype(jnp.bfloat16).reshape(groups, part, head_dim)
+            stage[h // bunch, :, c, :, inside] = total.astype(jnp.bfloat16).reshape(
+                groups, part, head_dim
+            )
+
+        @pl.when(lax.rem(h, bunch) == bunch - 1)
+        def _():
+            for d in order:
+                push(h // bunch, d).start()
+
+        land[:, :, columns_of(group, h)] = stage[h // bunch, group, :, :, inside]
+
+    @pl.loop(0, bunches)
+    def _(b):
         for d in order:
-            push(h, d).start()
-        land[:, :, columns_of(group, h)] = stage[h, group]
-
-    @pl.loop(0, heads)
-    def _(h):
-        for d in order:
-            push(h, d).wait_recv()
+            push(b, d).wait_recv()
 
     pltpu.make_async_copy(sums, sums, mate_send).wait()
     pltpu.make_async_copy(gathered, gathered, sum_send).wait()
@@ -310,6 +322,7 @@
     shards = lax.axis_size("seq")
     groups = lax.axis_size("head")
     part = length // groups
+    bunch = 2 if heads % 2 == 0 else 1
     docs = doc_lengths.shape[0]
     hbm = pl.BlockSpec(memory_space=pltpu.HBM)
     vmem = pl.BlockSpec(memory_space=pltpu.VMEM)
@@ -330,7 +343,7 @@
             pltpu.VMEM((heads, 2, head_dim // 2, head_dim), f32),
             pltpu.VMEM((heads, shards // 2 - 1, 2, head_dim // 2, head_dim), f32),
             pltpu.VMEM((3, length, head_dim), f32),
-            pltpu.VMEM((heads, groups, 3, part, head_dim), bf16),
+            pltpu.VMEM((heads // bunch, groups, 3, part, bunch * head_dim), bf16),
             pltpu.SMEM((2, shards // 2 + 2), f32),
             pltpu.SemaphoreType.DMA((heads,)),
             pltpu.SemaphoreType.DMA,
@@ -338,7 +351,7 @@
             pltpu.SemaphoreType.DMA,
             pltpu.SemaphoreType.DMA((heads,)),
             pltpu.SemaphoreType.DMA,
-            pltpu.SemaphoreType.DMA((groups - 1, heads)),
+            pltpu.SemaphoreType.DMA((groups - 1, heads // bunch)),
             pltpu.SemaphoreType.DMA((2,)),
         ],
         compiler_params=pltpu.CompilerParams(

time: 151 us -> 154 us (1.020); the launches traced: 151 us -> 151 us
  no operation moved by 1% of the time
where the time goes in v9:
time: 154 us; the launch traced here: 151 us
  Pallas kernels  151 us (98%)
    pallas_call x1, Pallas kernels, body(): pl.pallas_call(functools.partial(kernel, shards, groups, docs), out_shape...  148 us

profile of v9, /device:TPU:0, one launch (start us, length us, event | category | flops | bytes accessed | tf_op | source)
XLA Modules:
  0.0 151.4 jit_solution(7731869650501646450)
XLA Ops:
  0.6 148.0 %shard_map.85.land = bf16[3,128,8192]{2,1,0:T(8,128)(2,1)S(1)} custom-call(s32[8]{0:T(128)} %lengths_hbm.1, f32[16]{0:T(128)} %rates_hbm.1, bf16[512,2048]{1,0:T(8,128)(2,1)} %q_hbm.1, bf16[512,2048]{1,0:T(8,128)(2,1)} %k_hbm.1, bf16[512,2048]{1,0:T(8,128)(2,1)} %v_hbm.1, bf16[512,2048]{1,0:T(8,128)(2,1)} %g_hbm.1), custom_call_target="tpu_custom_call" | custom-call | flops 6710886400 | bytes 14680064 | tf_op jit(solution)/shard_map/pallas_call | solution.py:330
  148.6 2.8 %shard_map.86 = (bf16[128,8192]{1,0:T(8,128)(2,1)}, bf16[128,8192]{1,0:T(8,128)(2,1)}, bf16[128,8192]{1,0:T(8,128)(2,1)}) custom-call(bf16[3,128,8192]{2,1,0:T(8,128)(2,1)S(1)} %shard_map.85.land), custom_call_target="tpu_custom_call" | custom-call | tf_op jit(solution)/shard_map/pallas_call | solution.py:367

commit v10 on v4

--- a/solution.py
+++ b/solution.py
@@ -67,13 +67,6 @@
             for i, ref in enumerate(inputs)
         ]
 
-    small = [
-        pltpu.make_async_copy(lengths_hbm, lengths, small_sem.at[0]),
-        pltpu.make_async_copy(rates_hbm, rates, small_sem.at[1]),
-    ]
-    for copy in small + load(0) + load(1):
-        copy.start()
-
     barrier = pltpu.get_barrier_semaphore()
     for d in range(1, shards):
         peer = lax.rem(shard + d, shards)
@@ -81,6 +74,13 @@
     for d in range(1, groups):
         peer = lax.rem(group + d, groups)
         pl.semaphore_signal(barrier, inc=1, device_id=(shard, peer), device_id_type=MESH)
+
+    small = [
+        pltpu.make_async_copy(lengths_hbm, lengths, small_sem.at[0]),
+        pltpu.make_async_copy(rates_hbm, rates, small_sem.at[1]),
+    ]
+    for copy in small + load(0) + load(1):
+        copy.start()
 
     first = shard * length
     for copy in small:
@@ -157,6 +157,8 @@
                 ).start()
 
     summarise(0)
+    pl.semaphore_wait(barrier, shards + groups - 2)
+    swap(0).start()
 
     row_dist[2] = jnp.where(segment == seg_prev, where + 1.0, NEVER)
     row_dist[3] = jnp.where(segment == seg_next, length - where, NEVER)
@@ -199,11 +201,9 @@
     gaps[1, pairs] = jnp.where(is_left, 0.0, step_bwd)
     gaps[1, pairs + 1] = jnp.where(is_left, step_bwd, 0.0)
 
-    pl.semaphore_wait(barrier, shards + groups - 2)
-    swap(0).start()
+    send_sums(0)
     summarise(1)
     swap(1).start()
-    send_sums(0)
 
     order = sorted(range(1, groups), key=lambda d: abs(2 * d - groups))
 

time: 151 us -> 151 us (level)
  no operation moved by 1% of the time
where the time goes in v10:
time: 151 us
  Pallas kernels  150 us (99%)
    pallas_call x1, Pallas kernels, body(): pl.pallas_call(functools.partial(kernel, shards, groups, docs), out_shape...  147 us

profile of v10, /device:TPU:0, one launch (start us, length us, event | category | flops | bytes accessed | tf_op | source)
XLA Modules:
  0.0 150.8 jit_solution(7285998879469336441)
XLA Ops:
  0.6 147.4 %shard_map.85.land = bf16[3,128,8192]{2,1,0:T(8,128)(2,1)S(1)} custom-call(s32[8]{0:T(128)} %lengths_hbm.1, f32[16]{0:T(128)} %rates_hbm.1, bf16[512,2048]{1,0:T(8,128)(2,1)} %q_hbm.1, bf16[512,2048]{1,0:T(8,128)(2,1)} %k_hbm.1, bf16[512,2048]{1,0:T(8,128)(2,1)} %v_hbm.1, bf16[512,2048]{1,0:T(8,128)(2,1)} %g_hbm.1), custom_call_target="tpu_custom_call" | custom-call | flops 6710886400 | bytes 14680064 | tf_op jit(solution)/shard_map/pallas_call | solution.py:317
  148.0 2.8 %shard_map.86 = (bf16[128,8192]{1,0:T(8,128)(2,1)}, bf16[128,8192]{1,0:T(8,128)(2,1)}, bf16[128,8192]{1,0:T(8,128)(2,1)}) custom-call(bf16[3,128,8192]{2,1,0:T(8,128)(2,1)S(1)} %shard_map.85.land), custom_call_target="tpu_custom_call" | custom-call | tf_op jit(solution)/shard_map/pallas_call | solution.py:354
